TPU v7x, 32 devices: a whole 2x2x4 slice. The times are simulated.
32 devices in a mesh: dp: 8 (over z, x), fsdp: 4 (over y, core).
Axes of the slice: x: 2, y: 2, z: 4, core: 2. Of those that a mesh axis runs over, the one named last changes fastest.
Arguments:
- tokens: bfloat16 [128, 256, 512], P(('dp', 'fsdp')), may hold values from -6 to 6
- cotangent: bfloat16 [128, 256, 512], P(('dp', 'fsdp')), may hold values from -6 to 6
- reveal_order: int32 [128, 256], P(('dp', 'fsdp')), may hold values from 0 to 255, each once within a row
- reveal_step: int32 [128], P(('dp', 'fsdp')), may hold values from 1 to 256
- lengths: int32 [128], P(('dp', 'fsdp')), may hold values from 224 to 256
- weight_qkv: float32 [512, 1536], P(('dp', 'fsdp')), may hold values from -0.25 to 0.25
- weight_out: float32 [512, 512], P(('dp', 'fsdp')), may hold values from -1 to 1
- weight_up: float32 [512, 2048], P(('dp', 'fsdp')), may hold values from -0.25 to 0.25
- weight_down: float32 [2048, 512], P(('dp', 'fsdp')), may hold values from -0.125 to 0.125
- vectors: float32 [5, 512], P(None, ('dp', 'fsdp')), may hold values from -4 to 4, as said below
- moment_qkv: float32 [512, 1536], P(('dp', 'fsdp')), may hold values from -64 to 64
- square_qkv: float32 [512, 1536], P(('dp', 'fsdp')), may hold values from 8.192 to 32.768
- moment_out: float32 [512, 512], P(('dp', 'fsdp')), may hold values from -20 to 20
- square_out: float32 [512, 512], P(('dp', 'fsdp')), may hold values from 0.73728 to 2.94912
- moment_up: float32 [512, 2048], P(('dp', 'fsdp')), may hold values from -32 to 32
- square_up: float32 [512, 2048], P(('dp', 'fsdp')), may hold values from 2.94912 to 11.79648
- moment_down: float32 [2048, 512], P(('dp', 'fsdp')), may hold values from -64 to 64
- square_down: float32 [2048, 512], P(('dp', 'fsdp')), may hold values from 11.79648 to 47.18592
- moment_vec: float32 [5, 512], P(None, ('dp', 'fsdp')), may hold values from -64 to 64
- square_vec: float32 [5, 512], P(None, ('dp', 'fsdp')), may hold values from 11.79648 to 47.18592
Outputs:
- block_output: bfloat16 [128, 256, 512], P(('dp', 'fsdp'))
- input_grad: float32 [128, 256, 512], P(('dp', 'fsdp'))
- new_moment_qkv: float32 [512, 1536], P(('dp', 'fsdp'))
- new_square_qkv: float32 [512, 1536], P(('dp', 'fsdp'))
- new_weight_qkv: float32 [512, 1536], P(('dp', 'fsdp'))
- new_moment_out: float32 [512, 512], P(('dp', 'fsdp'))
- new_square_out: float32 [512, 512], P(('dp', 'fsdp'))
- new_weight_out: float32 [512, 512], P(('dp', 'fsdp'))
- new_moment_up: float32 [512, 2048], P(('dp', 'fsdp'))
- new_square_up: float32 [512, 2048], P(('dp', 'fsdp'))
- new_weight_up: float32 [512, 2048], P(('dp', 'fsdp'))
- new_moment_down: float32 [2048, 512], P(('dp', 'fsdp'))
- new_square_down: float32 [2048, 512], P(('dp', 'fsdp'))
- new_weight_down: float32 [2048, 512], P(('dp', 'fsdp'))
- new_moment_vec: float32 [5, 512], P(None, ('dp', 'fsdp'))
- new_square_vec: float32 [5, 512], P(None, ('dp', 'fsdp'))
- new_vectors: float32 [5, 512], P(None, ('dp', 'fsdp'))
Inputs may be any that keep to these rules, and one draw needn't show every extreme that they name: `vectors`: rows 0 and 1 lie in 0.7 to 1.3.
All inputs are finite; a program needn't handle non-finite values.
Results may differ from a plain program's by a relative error of at most 0.0085.
The roundings to bfloat16 on the way count: a program that leaves them out, or rounds other values in their place, can miss the bound.
Values may be sent and summed in bfloat16 or wider, within the bound.
No kernel may reach another device: no remote copies, remote signals or barrier semaphores. Data moves between devices by JAX's collectives and lax.ppermute only.
A program may use at most 128 MiB of HBM per device.

v0:
```python
import functools

import jax
import jax.numpy as jnp
from jax import lax
from jax.experimental import pallas as pl
from jax.experimental.pallas import tpu as pltpu
from jax.sharding import PartitionSpec as P

D = 512
HEADS = 8
HEAD = 64
FF = 2048
QUARTER = FF // 4
LANES = 128
PAIRS = D // LANES
ROWS = 16
STEP = 10
AXES = ("dp", "fsdp")
SCALE = 1.2
NEAR_PARTS = 3
UNROLL = 2
VMEM_BYTES = 16 * 1024 * 1024

norm_epsilon = 1e-05
beta_first = 0.9
beta_second = 0.999
adam_epsilon = 1e-08
weight_decay = 0.1
matrix_rate = 0.02
output_rate = 0.1
vector_rate = 0.2
masked_score = -1000000000.0
gelu_scale = 0.7978845608028654
gelu_cubic = 0.044715
FIRST_PAD = 224


def low(values):
    return values.astype(jnp.bfloat16)


def wide(values):
    return values.astype(jnp.float32)


def dot(left, right):
    return lax.dot_general(left, right, (((1,), (0,)), ((), ())), preferred_element_type=jnp.float32)


def dot_rows(left, right):
    return lax.dot_general(left, right, (((1,), (1,)), ((), ())), preferred_element_type=jnp.float32)


def dot_columns(left, right):
    return lax.dot_general(left, right, (((0,), (0,)), ((), ())), preferred_element_type=jnp.float32)


def cost(micros):
    return pl.CostEstimate(flops=int(micros * SCALE * 1.15e9), bytes_accessed=0, transcendentals=0)


class Refs:
    pass


def call(body, name, micros, ins, outs, scratch=(), reused=()):
    in_names, out_names = [entry[0] for entry in ins], [entry[0] for entry in outs]
    aliases = {in_names.index(taken): out_names.index(given) for taken, given in reused}
    names = [entry[0] for entry in ins] + [entry[0] for entry in outs] + [entry[0] for entry in scratch]

    def kernel(*refs):
        named = Refs()
        for entry, ref in zip(names, refs):
            setattr(named, entry, ref)
        body(named)

    results = pl.pallas_call(
        kernel,
        out_shape=[jax.ShapeDtypeStruct(shape, kind) for _, shape, kind in outs],
        in_specs=[entry[2] if len(entry) > 2 else whole() for entry in ins],
        out_specs=[whole() for _ in outs],
        scratch_shapes=[pltpu.VMEM(shape, kind) for _, shape, kind in scratch],
        compiler_params=pltpu.CompilerParams(vmem_limit_bytes=VMEM_BYTES),
        cost_estimate=cost(micros),
        input_output_aliases=aliases,
        name=name,
    )(*[entry[1] for entry in ins])
    out = Refs()
    for entry, value in zip(outs, results):
        setattr(out, entry[0], value)
    return out


def whole():
    return pl.BlockSpec(memory_space=pltpu.VMEM)


def scalars():
    return pl.BlockSpec(memory_space=pltpu.SMEM)


FAR = (0, 8, 16, 24)


def block_device(me, core, place):
    first = jnp.where(core == 0, 4, 2)
    near = (0, first, 6 - first, 6)[place // len(FAR)]
    return me ^ near ^ FAR[place % len(FAR)]


def assemble(me, stacks, targets):
    for stream in range(2):
        for upper in range(2):
            stack = stacks[2 * stream + upper]
            for place in range(8):
                device = block_device(me ^ stream, (me & 1) ^ stream, place + upper * 8)
                rows = pl.ds(pl.multiple_of(device * ROWS, ROWS), ROWS)
                for ref, column in targets:
                    ref[rows, :] = stack[pl.ds(place * ROWS, ROWS), pl.ds(column, ref.shape[1])]


def arrange(me, sources, keep_ref, send_ref):
    for place in range(16):
        here = pl.ds(place * ROWS, ROWS)
        for stream, out in ((0, keep_ref), (1, send_ref)):
            device = block_device(me ^ stream, (me & 1) ^ stream, place)
            rows = pl.ds(pl.multiple_of(device * ROWS, ROWS), ROWS)
            at = 0
            for ref in sources:
                out[here, pl.ds(at, ref.shape[1])] = ref[rows, :].astype(out.dtype)
                at += ref.shape[1]


def arranged(columns):
    shape = (16 * ROWS, columns)
    return [("keep", shape, jnp.float32), ("send", shape, jnp.bfloat16)]


def centre(values):
    centred = values - jnp.mean(values, axis=-1, keepdims=True)
    scale = lax.rsqrt(jnp.mean(centred * centred, axis=-1, keepdims=True) + norm_epsilon)
    return centred * scale, scale


def norm_back(grad, gain, hat, scale):
    inner = grad * gain
    return scale * (
        inner - jnp.mean(inner, axis=-1, keepdims=True) - hat * jnp.mean(inner * hat, axis=-1, keepdims=True)
    )


def masked_rows(order_row, step):
    seq = order_row.shape[1]
    flags = jnp.where(order_row >= step, 1.0, 0.0)
    column = jnp.transpose(jnp.broadcast_to(flags, (LANES, seq)))
    return jnp.concatenate([column] * (D // LANES), axis=1) > 0.5


def pair_split(pair, scale=None):
    lane = lax.broadcasted_iota(jnp.int32, pair.shape, 1)
    values = wide(pair)
    if scale is not None:
        values = values * scale
    return jnp.concatenate([low(jnp.where(lane < HEAD, values, 0.0)), low(jnp.where(lane < HEAD, 0.0, values))], axis=0)


def key_scores(keys, both_queries, length):
    scores = dot_rows(keys, both_queries)
    seq = scores.shape[0]
    tail = scores[FIRST_PAD:]
    row = lax.broadcasted_iota(jnp.int32, tail.shape, 0) + FIRST_PAD
    return jnp.concatenate([scores[:FIRST_PAD], jnp.where(row < length, tail, masked_score)], axis=0)


def load_input(r, span, rows):
    masked = masked_rows(r.order[span], r.step[span])
    return masked, jnp.where(masked, r.vec[4:5, :], wide(r.tokens[rows, :]))


def each_span(seq, spans, body):
    def step(index, carry):
        span = spans[0] + index
        body(span, pl.ds(pl.multiple_of(span * seq, seq), seq))
        return carry

    lax.fori_loop(0, len(spans), step, 0, unroll=UNROLL)


def attention(scalar, order, tokens, first, spans, front=None):
    count, _, seq = order.shape
    fresh = front is None

    def body(r):
        if fresh:
            stacks = (r.stack0, r.stack1, r.stack2, r.stack3)
            assemble(r.me[0], stacks, ((r.weight, 0), (r.columns, 3 * D)))
            r.vec[...] = jnp.transpose(wide(r.columns[...]))[:8]
        else:
            for name in ("normed", "p", "attended"):
                old = getattr(r, "front_" + name)
                getattr(r, name)[pl.ds(0, old.shape[0]), :] = old[...]
            r.logs[: spans[0]] = r.front_logs[...]

        def one_span(span, rows):
            started = load_input(r, span, rows)[1]
            normed = low(centre(started)[0] * r.vec[0:1, :] + r.vec[2:3, :])
            r.normed[rows, :] = normed
            r.p[rows, :] = low(dot(normed, r.weight[...]))
            for pair in range(PAIRS):
                lanes = pl.ds(pair * LANES, LANES)
                queries = pair_split(r.p[rows, lanes], HEAD**-0.5)
                scores = key_scores(r.p[rows, pl.ds(D + pair * LANES, LANES)], queries, r.length[span])
                peak = jnp.max(scores, axis=0, keepdims=True)
                exped = jnp.exp(scores - peak)
                total = jnp.sum(exped, axis=0, keepdims=True)
                probability = low(exped / total)
                r.logs[span, pair : pair + 1, :] = peak + jnp.log(total)
                values = jnp.transpose(r.p[rows, pl.ds(2 * D + pair * LANES, LANES)])
                attended = jnp.concatenate(
                    [dot(values[:HEAD], probability[:, :seq]), dot(values[HEAD:], probability[:, seq:])], axis=0
                )
                r.attended[rows, lanes] = jnp.transpose(low(attended))

        each_span(seq, spans, one_span)

    ins = [(name, array, scalars()) for name, array in scalar.items()] + [("order", order), ("tokens", tokens)]
    count = spans[-1] + 1
    rows = count * seq
    outs = [
        ("normed", (rows, D), jnp.bfloat16),
        ("p", (rows, 3 * D), jnp.bfloat16),
        ("attended", (rows, D), jnp.bfloat16),
        ("logs", (count, PAIRS, 2 * seq), jnp.float32),
    ]
    scratch = []
    if fresh:
        ins += [("stack%d" % n, stack) for n, stack in enumerate(first)]
        outs += [("weight", (D, 3 * D), jnp.bfloat16), ("vec", (8, D), jnp.float32)]
        scratch = [("columns", (D, LANES), jnp.bfloat16)]
    else:
        ins += [("weight", front.weight), ("vec", front.vec)]
        ins += [("front_" + name, getattr(front, name)) for name in ("normed", "p", "attended", "logs")]
    return call(body, "attention", 3 * len(spans), ins, outs, scratch)


def hidden_quarter(normed, upstream, up, down):
    hidden = dot(normed, up)
    grad_act = dot_rows(upstream, down)
    squared = hidden * hidden
    tilt = jnp.tanh(hidden * (gelu_scale + (gelu_scale * gelu_cubic) * squared))
    gate = 0.5 + 0.5 * tilt
    active = hidden * gate
    slope = gate + active * (1.0 - tilt) * (gelu_scale + (3.0 * gelu_scale * gelu_cubic) * squared)
    grad_hidden = low(grad_act * slope)
    return low(active), grad_hidden, dot_rows(grad_hidden, up)


def quarter_call(quarter, scalar, cotangent, stacks, ins, outs, seq, before, after, micros, reused=(), mate=None):
    total = cotangent.shape[0]
    column = 2 * QUARTER * (quarter % 2)

    def body(r):
        stacks = (r.stack0, r.stack1, r.stack2, r.stack3)
        targets = [(r.up, column), (r.down_full, column + QUARTER)]
        if quarter == 0:
            targets.append((r.out_full, 4 * QUARTER))
        assemble(r.me[0], stacks, targets)

        def one_span(span, rows):
            normed = before(r, span, rows)
            active, grad_hidden, back = hidden_quarter(normed, r.cot[rows, :], r.up[...], r.down_full[...])
            r.active[rows, :] = active
            r.grad_hidden[rows, :] = grad_hidden
            after(r, rows, back)

        each_span(seq, range(total // seq), one_span)
        r.grad_up[...] = dot_columns(r.middle_normed[...], r.grad_hidden[...])
        r.grad_down[...] = dot_columns(r.active[...], r.cot[...])
        if mate is not None:
            arrange(r.me[0], (r.mate_up, r.mate_down, r.grad_up, r.grad_down), r.keep, r.send)

    ins = [("me", scalar["me"], scalars()), ("cot", cotangent)] + ins
    ins += [("stack%d" % n, stack) for n, stack in enumerate(stacks)]
    outs = outs + [("active", (total, QUARTER), jnp.bfloat16), ("down_full", (QUARTER, D), jnp.bfloat16)]
    grads = [("grad_up", (D, QUARTER), jnp.float32), ("grad_down", (QUARTER, D), jnp.float32)]
    scratch = [("up", (D, QUARTER), jnp.bfloat16), ("grad_hidden", (total, QUARTER), jnp.bfloat16)]
    if mate is None:
        outs = outs + grads
    else:
        ins += [("mate_up", mate.grad_up), ("mate_down", mate.grad_down)]
        outs = outs + arranged(4 * QUARTER)
        scratch = scratch + grads
    return call(body, "hidden%d" % quarter, micros, ins, outs, scratch, reused)


def first_quarter(scalar, order, tokens, cotangent, vec, attended, stacks):
    seq = order.shape[2]
    total = tokens.shape[0]

    def enter(r, span, rows):
        middle = load_input(r, span, rows)[1] + dot(r.attended[rows, :], r.out_full[...])
        r.middle[rows, :] = middle
        normed = low(centre(middle)[0] * r.vec[1:2, :] + r.vec[3:4, :])
        r.middle_normed[rows, :] = normed
        return normed

    def leave(r, rows, back):
        r.back[rows, :] = back

    ins = [("step", scalar["step"], scalars()), ("order", order), ("tokens", tokens), ("vec", vec), ("attended", attended)]
    outs = [("middle", (total, D), jnp.float32), ("middle_normed", (total, D), jnp.bfloat16)]
    outs += [("back", (total, D), jnp.float32), ("out_full", (D, D), jnp.bfloat16)]
    return quarter_call(0, scalar, cotangent, stacks, ins, outs, seq, enter, leave, 8.5)


def next_quarter(quarter, scalar, cotangent, stacks, normed, back, seq, mate=None):
    total = normed.shape[0]

    def take(r, span, rows):
        return r.middle_normed[rows, :]

    def leave(r, rows, back):
        r.back[rows, :] = r.old_back[rows, :] + back

    ins = [("middle_normed", normed), ("old_back", back)]
    outs = [("back", (total, D), jnp.float32)]
    reused = [("old_back", "back")]
    return quarter_call(quarter, scalar, cotangent, stacks, ins, outs, seq, take, leave, 6.5, reused, mate)


def middle_back(scalar, cotangent, vec, attended, middle, back, out_full, seq, quarters):
    total = middle.shape[0]

    def body(r):
        r.dvec[...] = jnp.zeros_like(r.dvec)

        def one_span(span, rows):
            back = r.back[rows, :]
            hat, scale = centre(r.middle[rows, :])
            dmiddle = wide(r.cot[rows, :]) + norm_back(back, r.vec[1:2, :], hat, scale)
            r.dmiddle[rows, :] = dmiddle
            r.dvec[1:2, :] += jnp.sum(back * hat, axis=0, keepdims=True)
            r.dvec[3:4, :] += jnp.sum(back, axis=0, keepdims=True)
            mixed = low(dmiddle)
            r.mixed[rows, :] = mixed
            r.dattended[rows, :] = low(dot_rows(mixed, r.out_full[...]))

        each_span(seq, range(total // seq), one_span)
        r.grad_out[...] = dot_columns(r.attended[...], r.mixed[...])
        arrange(r.me[0], (r.up0, r.down0, r.up1, r.down1, r.grad_out), r.keep, r.send)

    ins = [("me", scalar["me"], scalars()), ("cot", cotangent), ("vec", vec), ("attended", attended)]
    ins += [("middle", middle), ("back", back), ("out_full", out_full)]
    for n, quarter in enumerate(quarters):
        ins += [("up%d" % n, quarter.grad_up), ("down%d" % n, quarter.grad_down)]
    outs = [("dmiddle", (total, D), jnp.float32), ("dattended", (total, D), jnp.bfloat16), ("dvec", (8, D), jnp.float32)]
    outs += arranged(4 * QUARTER + D)
    scratch = [("grad_out", (D, D), jnp.float32), ("mixed", (total, D), jnp.bfloat16)]
    return call(body, "middle_back", 4, ins, outs, scratch)


def branch_output(middle, quarters, seq, spans, front=None):
    def body(r):
        if front is not None:
            r.result[pl.ds(0, front.shape[0]), :] = r.front[...]

        def one_span(span, rows):
            result = r.middle[rows, :]
            for n in range(4):
                result = result + dot(getattr(r, "active%d" % n)[rows, :], getattr(r, "down%d" % n)[...])
            r.result[rows, :] = low(result)

        each_span(seq, spans, one_span)

    ins = [("middle", middle)]
    for n, quarter in enumerate(quarters):
        ins += [("active%d" % n, quarter.active), ("down%d" % n, quarter.down_full)]
    if front is not None:
        ins += [("front", front)]
    return call(body, "branch_output", 25, ins, [("result", ((spans[-1] + 1) * seq, D), jnp.bfloat16)]).result


def attention_back(scalar, pair, normed, p, logs, dattended, seq, mate=None):
    total = normed.shape[0]
    last = pair == PAIRS - 1

    def body(r):
        def one_span(span, rows):
            queries = pair_split(r.p[rows, pl.ds(pair * LANES, LANES)], HEAD**-0.5)
            dattended = pair_split(r.dattended[rows, pl.ds(pair * LANES, LANES)])
            keys = r.p[rows, pl.ds(D + pair * LANES, LANES)]
            scores = key_scores(keys, queries, r.length[span])
            probability = jnp.exp(scores - r.logs[span, pair : pair + 1, :])
            dprobability = dot_rows(r.p[rows, pl.ds(2 * D + pair * LANES, LANES)], dattended)
            inner = jnp.sum(probability * dprobability, axis=0, keepdims=True)
            dscores = low(probability * (dprobability - inner))
            dvalues = low(dot(low(probability), dattended))
            dkeys = low(dot(dscores, queries))
            keys = jnp.transpose(low(wide(keys) * HEAD**-0.5))
            dqueries = jnp.concatenate([dot(keys[:HEAD], dscores[:, :seq]), dot(keys[HEAD:], dscores[:, seq:])], axis=0)
            r.dp[rows, :] = jnp.concatenate([jnp.transpose(low(dqueries)), dkeys, dvalues], axis=1)

        each_span(seq, range(total // seq), one_span)
        if not last:
            r.grad[...] = dot_columns(r.normed[...], r.dp[...])
        if mate is not None:
            arrange(r.me[0], (r.mate, r.grad), r.keep, r.send)

    ins = [("me", scalar["me"], scalars()), ("length", scalar["length"], scalars())]
    ins += [("normed", normed), ("p", p), ("logs", logs), ("dattended", dattended)]
    outs = [("dp", (total, 3 * LANES), jnp.bfloat16)]
    grad = ("grad", (D, 3 * LANES), jnp.float32)
    scratch = []
    if mate is not None:
        ins += [("mate", mate.grad)]
        outs += arranged(6 * LANES)
        scratch = [grad]
    elif not last:
        outs += [grad]
    return call(body, "attention_back", 4.6, ins, outs, scratch)


def input_back(scalar, order, tokens, vec, normed, dmiddle, weight, dvec, parts):
    seq = order.shape[2]
    total = tokens.shape[0]

    def body(r):
        parts = [getattr(r, "dp%d" % n) for n in range(PAIRS)]
        r.dvec[...] = jnp.zeros_like(r.dvec)
        r.dvec[:8, :] = r.dvec_in[...]

        def one_span(span, rows):
            dp = [part[rows, pl.ds(kind * LANES, LANES)] for kind in range(3) for part in parts]
            back = dot_rows(jnp.concatenate(dp, axis=1), r.weight[...])
            masked, started = load_input(r, span, rows)
            hat, scale = centre(started)
            dstarted = r.dmiddle[rows, :] + norm_back(back, r.vec[0:1, :], hat, scale)
            r.input_grad[rows, :] = jnp.where(masked, 0.0, dstarted)
            r.dvec[0:1, :] += jnp.sum(back * hat, axis=0, keepdims=True)
            r.dvec[2:3, :] += jnp.sum(back, axis=0, keepdims=True)
            r.dvec[4:5, :] += jnp.sum(jnp.where(masked, dstarted, 0.0), axis=0, keepdims=True)

        each_span(seq, range(total // seq), one_span)
        r.columns[...] = jnp.transpose(r.dvec[...])
        r.grad[...] = dot_columns(r.normed[...], parts[-1][...])
        arrange(r.me[0], (r.mate, r.grad, r.columns), r.keep, r.send)

    ins = [("me", scalar["me"], scalars()), ("step", scalar["step"], scalars()), ("order", order), ("tokens", tokens)]
    ins += [("vec", vec), ("dmiddle", dmiddle), ("normed", normed), ("weight", weight), ("dvec_in", dvec)]
    ins += [("dp%d" % n, part.dp) for n, part in enumerate(parts)]
    ins += [("mate", parts[-2].grad)]
    outs = [("input_grad", (total, D), jnp.float32)] + arranged(7 * LANES)
    scratch = [
        ("dvec", (LANES, D), jnp.float32),
        ("columns", (D, LANES), jnp.float32),
        ("grad", (D, 3 * LANES), jnp.float32),
    ]
    return call(body, "input_back", 6.5, ins, outs, scratch)


def fold_kernel(keep_ref, taken_ref, total_ref, send_ref):
    half = total_ref.shape[0]
    total_ref[...] = keep_ref[:half, :] + wide(taken_ref[:half, :])
    send_ref[...] = low(keep_ref[half:, :] + wide(taken_ref[half:, :]))


def fold(keep, taken):
    rows, columns = keep.shape
    return pl.pallas_call(
        fold_kernel,
        out_shape=(
            jax.ShapeDtypeStruct((rows // 2, columns), jnp.float32),
            jax.ShapeDtypeStruct((rows // 2, columns), jnp.bfloat16),
        ),
        in_specs=[whole()] * 2,
        out_specs=(whole(), whole()),
        compiler_params=pltpu.CompilerParams(vmem_limit_bytes=VMEM_BYTES),
        cost_estimate=cost(1),
        name="fold",
    )(keep, taken)


def adam_update(master, gradient, moment, square, step_rate, decay_rate):
    moment_new = beta_first * moment + (1.0 - beta_first) * gradient
    square_new = beta_second * square + (1.0 - beta_second) * gradient * gradient
    corrected = (
        moment_new
        / (1.0 - beta_first**STEP)
        / (jnp.sqrt(square_new / (1.0 - beta_second**STEP)) + adam_epsilon)
    )
    return (moment_new, square_new, master - step_rate * (corrected + decay_rate * master))


def unit_order():
    unit = lax.broadcasted_iota(jnp.int32, (D, D), 0)
    place = lax.broadcasted_iota(jnp.int32, (D, D), 1)
    wanted = (place % LANES // ROWS) * 64 + (place // LANES) * ROWS + place % ROWS
    return jnp.where(unit == wanted, 1.0, 0.0).astype(jnp.bfloat16)


def hidden_update_kernel(*refs):
    halves = (refs[0:4], refs[4:8])
    up, down, out = refs[8:11], refs[11:14], refs[14:17]
    new_up, new_down, new_out = refs[17:20], refs[20:23], refs[23:26]

    def summed(half, columns):
        return half[0][:ROWS, columns] + sum(wide(part[:, columns]) for part in half[1:])

    def update(new, old, index, grad, rate):
        results = adam_update(old[0][index], grad, old[1][index], old[2][index], rate, weight_decay)
        for ref, value in zip(new, results):
            ref[index] = value

    sort = unit_order()
    for group in range(FF // D):
        grads = []
        for quarter in range(4):
            columns = pl.ds((quarter % 2) * 2 * QUARTER + group * LANES, LANES)
            grads.append(summed(halves[quarter // 2], columns))
        rest = jnp.concatenate(grads, axis=1)
        grad = 0.0
        for _ in range(3):
            piece = low(rest)
            grad = grad + dot_rows(piece, sort)
            rest = rest - wide(piece)
        update(new_up, up, (slice(None), pl.ds(group * D, D)), grad, matrix_rate)
    for quarter in range(4):
        grad = summed(halves[quarter // 2], pl.ds((quarter % 2) * 2 * QUARTER + QUARTER, D))
        update(new_down, down, (pl.ds(quarter * ROWS, ROWS), slice(None)), grad, matrix_rate)
    update(new_out, out, Ellipsis, summed(halves[1], pl.ds(4 * QUARTER, D)), output_rate)


def hidden_update(total_one, parts_one, total_two, parts_two, up, down, out):
    outs = [jax.ShapeDtypeStruct(state[0].shape, jnp.float32) for state in (up, down, out) for _ in range(3)]
    results = pl.pallas_call(
        hidden_update_kernel,
        out_shape=outs,
        in_specs=[whole()] * 17,
        out_specs=[whole()] * 9,
        compiler_params=pltpu.CompilerParams(vmem_limit_bytes=VMEM_BYTES),
        cost_estimate=cost(3),
        name="hidden_update",
    )(total_one, *parts_one, total_two, *parts_two, *up, *down, *out)
    return results[:3], results[3:6], results[6:]


def last_update_kernel(*refs):
    early, late = refs[:4], refs[4:8]
    qkv, vec = refs[8:11], refs[11:14]
    new_qkv, new_vec = refs[14:17], refs[17:20]

    def summed(group, column):
        columns = pl.ds(column, LANES)
        return group[0][:ROWS, columns] + sum(wide(part[:, columns]) for part in group[1:])

    for pair in range(PAIRS):
        for kind in range(3):
            group, first = (early, 4 * QUARTER + D) if pair < 2 else (late, 0)
            grad = summed(group, first + (3 * (pair % 2) + kind) * LANES)
            here = pl.ds((kind * PAIRS + pair) * LANES, LANES)
            moment, square, master = adam_update(
                qkv[0][:, here], grad, qkv[1][:, here], qkv[2][:, here], matrix_rate, weight_decay
            )
            new_qkv[0][:, here], new_qkv[1][:, here], new_qkv[2][:, here] = moment, square, master
    grad = summed(late, 6 * LANES)
    grad = jnp.transpose(jnp.concatenate([grad, jnp.zeros((LANES - ROWS, LANES), jnp.float32)], axis=0))
    grad = grad[: vec[0].shape[0], :ROWS]
    results = adam_update(vec[0][...], grad, vec[1][...], vec[2][...], vector_rate, 0.0)
    for ref, value in zip(new_vec, results):
        ref[...] = value


def last_update(total_early, parts_early, total_late, parts_late, qkv, vec):
    outs = [jax.ShapeDtypeStruct(qkv[0].shape, jnp.float32)] * 3 + [jax.ShapeDtypeStruct(vec[0].shape, jnp.float32)] * 3
    results = pl.pallas_call(
        last_update_kernel,
        out_shape=outs,
        in_specs=[whole()] * 14,
        out_specs=[whole()] * 6,
        compiler_params=pltpu.CompilerParams(vmem_limit_bytes=VMEM_BYTES),
        cost_estimate=cost(1),
        name="last_update",
    )(total_early, *parts_early, total_late, *parts_late, *qkv, *vec)
    return results[:3], results[3:]


def exchange(values, count, even_mask, odd_mask):
    pairs = [(i, i ^ (odd_mask if i % 2 else even_mask)) for i in range(count)]
    return lax.ppermute(values, AXES, pairs)


def tie(value, *others):
    return lax.optimization_barrier((value, others))[0]


class Gather:
    def __init__(self, piece, count):
        self.piece, self.count, self.direct = piece, count, piece.shape[0] == ROWS
        self.parts, self.other = [], None

    def far(self):
        if self.direct:
            self.parts = [exchange(self.piece, self.count, offset, offset) for offset in FAR[1:]]
        return self.parts

    def split(self, columns):
        pair = [Gather(self.piece[:, :columns], self.count), Gather(self.piece[:, columns:], self.count)]
        parts = self.far()
        pair[0].parts = [part[:, :columns] for part in parts]
        pair[1].parts = [part[:, columns:] for part in parts]
        return pair

    def stack(self, *waits):
        if self.direct:
            self.piece = jnp.concatenate([self.piece] + [tie(part, *waits) for part in self.parts], axis=0)
        return self.piece

    def core(self, *waits):
        if not self.direct:
            return self.piece
        start = self.other.shape[0] if self.other is not None else 0
        taken = tie(exchange(self.piece[start:], self.count, 1, 1), *waits)
        self.other = taken if self.other is None else jnp.concatenate([self.other, taken], axis=0)
        return taken

    def near(self, *waits):
        if self.direct:
            taken = exchange(self.piece, self.count, 4, 2)
            self.piece = jnp.concatenate([self.piece, tie(taken, *waits)], axis=0)
        return self.piece

    def late(self, *waits):
        if self.direct:
            self.rest = tie(exchange(self.piece, self.count, 2, 4), *waits)

    def finish(self, *waits):
        if not self.direct:
            return ordered_stacks(self.piece)
        return (self.piece, self.rest, self.other, tie(exchange(self.rest, self.count, 1, 1), *waits))


class Scatter:
    def __init__(self, arranged, count, direct):
        self.total, self.send, self.count, self.direct = arranged.keep, arranged.send, count, direct

    def step(self, even, odd, *waits):
        if self.direct:
            self.total, self.send = fold(self.total, tie(exchange(self.send, self.count, even, odd), *waits))
        return self.total, self.send

    def core(self, *waits):
        return self.step(1, 1, *waits)

    def near(self, *waits):
        return self.step(2, 4, *waits)

    def next(self, *waits):
        if self.direct:
            self.total = self.total + wide(tie(exchange(self.send, self.count, 4, 2), *waits))
        return self.total

    def join(self, other):
        self.total = jnp.concatenate([self.total, other.total], axis=1)
        self.send = jnp.concatenate([self.send, other.send], axis=1)

    def parts(self, *waits):
        if not self.direct:
            return []
        taken = []
        for place in range(1, len(FAR)):
            part = low(self.total[place * ROWS : (place + 1) * ROWS])
            taken.append(tie(exchange(part, self.count, FAR[place], FAR[place]), *waits))
        return taken

    def full(self):
        return full_piece(self.total, self.send)


def split_units(up, down):
    rows, units = up.shape
    up = up.reshape(rows, units // 64, 4, ROWS)
    down = down.reshape(rows // ROWS, 4, ROWS, D)
    ups = [up[:, :, quarter].reshape(rows, units // 4) for quarter in range(4)]
    downs = [down[:, quarter].reshape(rows, D) for quarter in range(4)]
    return [jnp.concatenate([ups[n], downs[n], ups[n + 1], downs[n + 1]], axis=1) for n in (0, 2)]


def pack_kernel(*refs):
    sources, first, hidden, buffers, done = refs[:5], refs[5], refs[6], refs[7:12], refs[12]
    copies = [pltpu.make_async_copy(sources[n], buffers[n], done.at[n]) for n in range(5)]
    for copy in copies:
        copy.start()
    qkv, vec, out, up, down = buffers
    copies[0].wait()
    first[:, pl.ds(0, 3 * D)] = low(qkv[...])
    copies[1].wait()
    rows, columns = vec.shape
    turned = jnp.concatenate([vec[...], jnp.zeros((rows, LANES - columns), jnp.float32)], axis=1)
    turned = jnp.transpose(jnp.concatenate([turned, jnp.zeros((LANES - rows, LANES), jnp.float32)], axis=0))
    first[:, pl.ds(3 * D, LANES)] = low(turned[:ROWS])
    for copy in copies[2:]:
        copy.wait()
    sort = unit_order()
    for group in range(FF // D):
        mixed = low(dot(low(up[:, pl.ds(group * D, D)]), sort))
        for quarter in range(4):
            column = 2 * QUARTER * ((quarter + 2) % 4) + group * LANES
            hidden[:, pl.ds(column, LANES)] = mixed[:, quarter * LANES : (quarter + 1) * LANES]
    for quarter in range(4):
        rows = down[pl.ds(quarter * ROWS, ROWS), :]
        hidden[:, pl.ds(2 * QUARTER * ((quarter + 2) % 4) + QUARTER, D)] = low(rows)
    hidden[:, pl.ds(8 * QUARTER, D)] = low(out[...])


def pack(*sources):
    return pl.pallas_call(
        pack_kernel,
        out_shape=(
            jax.ShapeDtypeStruct((ROWS, 3 * D + LANES), jnp.bfloat16),
            jax.ShapeDtypeStruct((ROWS, 8 * QUARTER + D), jnp.bfloat16),
        ),
        in_specs=[pl.BlockSpec(memory_space=pl.ANY)] * 5,
        out_specs=(whole(), whole()),
        scratch_shapes=[pltpu.VMEM(source.shape, source.dtype) for source in sources] + [pltpu.SemaphoreType.DMA((5,))],
        compiler_params=pltpu.CompilerParams(vmem_limit_bytes=VMEM_BYTES),
        cost_estimate=cost(1),
        name="pack",
    )(*[pltpu.with_memory_space_constraint(source, pltpu.HBM) for source in sources])


def join_units(pieces):
    rows = pieces[0].shape[0]
    groups = [[piece[:, n * QUARTER : (n + 1) * QUARTER] for n in range(4)] for piece in pieces]
    ups = [groups[0][0], groups[0][2], groups[1][0], groups[1][2]]
    downs = [groups[0][1], groups[0][3], groups[1][1], groups[1][3]]
    up = jnp.stack([group.reshape(rows, QUARTER // ROWS, ROWS) for group in ups], axis=2)
    down = jnp.stack([group.reshape(rows // ROWS, ROWS, D) for group in downs], axis=1)
    return up.reshape(rows, 4 * QUARTER), down.reshape(rows * 4, D)


def stack_order(core):
    near = (0, 4, 2, 6) if core == 0 else (0, 2, 4, 6)
    return [core ^ group ^ offset for group in near for offset in FAR]


def ordered_stacks(piece):
    blocks = piece.reshape(32, ROWS, piece.shape[1])
    stacks = []
    for core in range(2):
        ordered = jnp.stack([blocks[device] for device in stack_order(core)])
        ordered = ordered.reshape(16 * ROWS, piece.shape[1])
        stacks += [ordered[: 8 * ROWS], ordered[8 * ROWS :]]
    return tuple(stacks)


def full_piece(keep, send):
    columns = keep.shape[1]
    blocks = jnp.concatenate([keep, wide(send)], axis=0).reshape(32, ROWS, columns)
    order = stack_order(0) + stack_order(1)
    return jnp.stack([blocks[order.index(device)] for device in range(32)]).reshape(32 * ROWS, columns)


def local(
    tokens,
    cotangent,
    reveal_order,
    reveal_step,
    lengths,
    weight_qkv,
    weight_out,
    weight_up,
    weight_down,
    vectors,
    moment_qkv,
    square_qkv,
    moment_out,
    square_out,
    moment_up,
    square_up,
    moment_down,
    square_down,
    moment_vec,
    square_vec,
):
    count = lax.axis_size("dp") * lax.axis_size("fsdp")
    direct = weight_qkv.shape[0] == ROWS and count == 32
    me = lax.axis_index("dp") * lax.axis_size("fsdp") + lax.axis_index("fsdp")
    me = (me if direct else 0 * me).astype(jnp.int32)[None]
    spans, seq = reveal_order.shape
    order = reveal_order.reshape(spans, 1, seq)
    flat = tokens.reshape(spans * seq, D)
    upstream = cotangent.reshape(spans * seq, D)

    if direct:
        piece_one, piece_rest = pack(weight_qkv, vectors, weight_out, weight_up, weight_down)
    else:
        columns = jnp.pad(low(vectors).T, ((0, 0), (0, LANES - vectors.shape[0])))
        halves = [jnp.concatenate([low(weight_qkv), columns], axis=1), low(weight_out), low(weight_up), low(weight_down)]
        piece_one, out, up, down = [lax.all_gather(half, AXES, axis=0, tiled=True) for half in halves]
        hidden = split_units(up, down)
        piece_rest = jnp.concatenate([hidden[1], hidden[0], out], axis=1)
    scalar = {"me": me, "step": reveal_step, "length": lengths}

    one = Gather(piece_one, count)
    one.far()
    one.stack()
    rest = Gather(tie(piece_rest, one.core()), count)
    three, two = rest.split(4 * QUARTER)
    one.near()
    one.late()
    one.core()
    first = one.finish()
    two.stack(*([one.rest] if direct else []))
    front = attention(scalar, order, flat, first, range(0, spans // 2))
    two.near(front.logs)
    two.late()
    two.core()
    three.stack(front.logs)
    rear = attention(scalar, order, tie(flat, two.piece), None, range(spans // 2, spans), front)
    vec, weight = front.vec, front.weight
    two.rest = tie(two.rest, rear.logs) if direct else None
    second = two.finish()
    three.near(rear.logs)
    h = [first_quarter(scalar, order, flat, tie(upstream, three.piece), vec, rear.attended, second)]
    normed = h[0].middle_normed
    three.late(h[0].back)
    three.core(h[0].back)
    h += [next_quarter(1, scalar, upstream, second, normed, h[0].back, seq, h[0])]
    third = three.finish(h[1].back)
    h += [next_quarter(2, scalar, upstream, third, normed, h[1].back, seq)]
    sum_one = Scatter(h[1], count, direct)
    h += [next_quarter(3, scalar, tie(upstream, *sum_one.core(h[2].back)), third, normed, h[2].back, seq)]
    turn = middle_back(
        scalar, tie(upstream, h[3].back), vec, rear.attended, h[0].middle, h[3].back, h[0].out_full, seq, h[2:]
    )
    sum_one.near(turn.dattended)
    sum_two = Scatter(turn, count, direct)

    def part(pair, *waits, mate=None):
        dattended = tie(turn.dattended, *waits)
        return attention_back(scalar, pair, rear.normed, rear.p, rear.logs, dattended, seq, mate)

    parts = [part(0, sum_one.total)]
    parts += [part(1, sum_one.next(parts[0].dp), *sum_two.core(parts[0].dp), mate=parts[0])]
    early = Scatter(parts[1], count, direct)
    parts += [part(2, sum_one.total)]
    parts_one = sum_one.parts(parts[2].dp)
    early.core(parts[2].dp)
    sum_two.near(parts[2].dp)
    parts += [part(3, sum_two.total, early.total, *parts_one)]
    early.near(parts[3].dp)
    if direct:
        sum_two.join(early)
    ready = tie(flat, parts[3].dp, sum_two.total)
    final = input_back(scalar, order, ready, vec, rear.normed, turn.dmiddle, weight, turn.dvec, parts)
    late = Scatter(final, count, direct)
    sum_two.next(final.input_grad)
    result = branch_output(tie(h[0].middle, sum_two.total), h, seq, range(0, spans // 2))
    late.core(result)
    result = branch_output(tie(h[0].middle, late.total), h, seq, range(spans // 2, spans), result)
    parts_two = sum_two.parts() if direct else []
    late.near(result, *parts_two[:NEAR_PARTS])
    qkv_state = (weight_qkv, moment_qkv, square_qkv)
    vec_state = (vectors, moment_vec, square_vec)
    out_state = (weight_out, moment_out, square_out)
    up_state = (weight_up, moment_up, square_up)
    down_state = (weight_down, moment_down, square_down)
    if direct:
        late.next(*parts_two)
        parts_late = late.parts()
        total_one = tie(sum_one.total, late.total)
        states = hidden_update(total_one, parts_one, sum_two.total, parts_two, up_state, down_state, out_state)
        new_up, new_down, new_out = states
        new_qkv, new_vec = last_update(sum_two.total, parts_two, late.total, parts_late, qkv_state, vec_state)
    else:
        ones, twos = sum_one.full(), sum_two.full()
        threes = jnp.concatenate([early.full(), late.full()], axis=1)
        qkv = [threes[:, (3 * pair + kind) * LANES :][:, :LANES] for kind in range(3) for pair in range(PAIRS)]
        grads = [jnp.concatenate(qkv, axis=1), threes[:, 3 * D : 3 * D + vectors.shape[0]]]
        grads += [twos[:, 4 * QUARTER :], *join_units([ones, twos])]
        grads = [lax.psum_scatter(grad, AXES, scatter_dimension=0, tiled=True) for grad in grads]

        def update(state, grad, rate, decay):
            return adam_update(state[0], grad, state[1], state[2], rate, decay)

        new_qkv = update(qkv_state, grads[0], matrix_rate, weight_decay)
        new_vec = update(vec_state, grads[1].T, vector_rate, 0.0)
        new_out = update(out_state, grads[2], output_rate, weight_decay)
        new_up = update(up_state, grads[3], matrix_rate, weight_decay)
        new_down = update(down_state, grads[4], matrix_rate, weight_decay)
    return (
        result.reshape(tokens.shape),
        final.input_grad.reshape(tokens.shape),
        *new_qkv,
        *new_out,
        *new_up,
        *new_down,
        *new_vec,
    )


def solution(mesh):
    return jax.shard_map(
        local,
        mesh=mesh,
        in_specs=(
            P(("dp", "fsdp"), None, None),
            P(("dp", "fsdp"), None, None),
            P(("dp", "fsdp"), None),
            P(("dp", "fsdp")),
            P(("dp", "fsdp")),
            P(("dp", "fsdp"), None),
            P(("dp", "fsdp"), None),
            P(("dp", "fsdp"), None),
            P(("dp", "fsdp"), None),
            P(None, ("dp", "fsdp")),
            P(("dp", "fsdp"), None),
            P(("dp", "fsdp"), None),
            P(("dp", "fsdp"), None),
            P(("dp", "fsdp"), None),
            P(("dp", "fsdp"), None),
            P(("dp", "fsdp"), None),
            P(("dp", "fsdp"), None),
            P(("dp", "fsdp"), None),
            P(None, ("dp", "fsdp")),
            P(None, ("dp", "fsdp")),
        ),
        out_specs=(
            P(("dp", "fsdp"), None, None),
            P(("dp", "fsdp"), None, None),
            P(("dp", "fsdp"), None),
            P(("dp", "fsdp"), None),
            P(("dp", "fsdp"), None),
            P(("dp", "fsdp"), None),
            P(("dp", "fsdp"), None),
            P(("dp", "fsdp"), None),
            P(("dp", "fsdp"), None),
            P(("dp", "fsdp"), None),
            P(("dp", "fsdp"), None),
            P(("dp", "fsdp"), None),
            P(("dp", "fsdp"), None),
            P(("dp", "fsdp"), None),
            P(None, ("dp", "fsdp")),
            P(None, ("dp", "fsdp")),
            P(None, ("dp", "fsdp")),
        ),
        check_vma=False,
    )
```

profile of v0, /device:TPU:0, one launch (start us, length us, event | category | flops | bytes accessed | tf_op | source)
XLA Modules:
  0.0 139.9 jit_solution(5243876041352525848)
XLA Ops:
  2.2 5.1 %collective-permute-start.2 = (bf16[16,1664]{1,0:T(8,128)(2,1)S(1)}, bf16[16,1664]{1,0:T(8,128)(2,1)S(1)}, u32[]{:S(2)}, u32[]{:S(2)}) collective-permute-start(bf16[16,1664]{1,0:T(8,128)(2,1)S(1)} %get-tuple-element.138), channel_id=1, source_target_pairs={{0,24},{1,25},{2,26},{3,27},{4,28},{5,29},{6,30},{7,31},{8,16},{9,... | collective-permute-start | bytes 159752 | tf_op jit(solution)/shard_map/ppermute | solution.py:590
  9.6 2.7 %collective-permute-done.1 = bf16[16,1664]{1,0:T(8,128)(2,1)S(1)} collective-permute-done((bf16[16,1664]{1,0:T(8,128)(2,1)S(1)}, bf16[16,1664]{1,0:T(8,128)(2,1)S(1)}, u32[]{:S(2)}, u32[]{:S(2)}) %collective-permute-start.1) | collective-permute-done | bytes 53280 | tf_op jit(solution)/shard_map/ppermute | solution.py:590
  15.4 2.4 %collective-permute-start.10 = (bf16[16,4608]{1,0:T(8,128)(2,1)S(1)}, bf16[16,4608]{1,0:T(8,128)(2,1)S(1)}, u32[]{:S(2)}, u32[]{:S(2)}) collective-permute-start(bf16[16,4608]{1,0:T(8,128)(2,1)S(1)} %get-tuple-element.139), channel_id=1, source_target_pairs={{0,24},{1,25},{2,26},{3,27},{4,28},{5,29},{6,30},{7,31},{8,16},{9,... | collective-permute-start | bytes 442376 | tf_op jit(solution)/shard_map/ppermute | solution.py:590
  21.5 2.5 %collective-permute-done.10 = bf16[16,4608]{1,0:T(8,128)(2,1)S(1)} collective-permute-done((bf16[16,4608]{1,0:T(8,128)(2,1)S(1)}, bf16[16,4608]{1,0:T(8,128)(2,1)S(1)}, u32[]{:S(2)}, u32[]{:S(2)}) %collective-permute-start.10) | collective-permute-done | bytes 147488 | tf_op jit(solution)/shard_map/ppermute | solution.py:590
  24.1 7.0 %collective-permute-done.9 = bf16[16,4608]{1,0:T(8,128)(2,1)S(1)} collective-permute-done((bf16[16,4608]{1,0:T(8,128)(2,1)S(1)}, bf16[16,4608]{1,0:T(8,128)(2,1)S(1)}, u32[]{:S(2)}, u32[]{:S(2)}) %collective-permute-start.9) | collective-permute-done | bytes 147488 | tf_op jit(solution)/shard_map/ppermute | solution.py:590
  33.1 5.1 %attention.2 = (bf16[512,512]{1,0:T(8,128)(2,1)S(1)}, bf16[512,1536]{1,0:T(8,128)(2,1)S(1)}, bf16[512,512]{1,0:T(8,128)(2,1)S(1)}, f32[2,4,512]{2,1,0:T(4,128)S(...) custom-call(s32[1]{0:T(128)} %bitcast.refs_0_, s32[4]{0:T(128)S(1)} %copy-done.18, s32[4]{0:T(128)S(1)} %copy-done.17, ...), custom_call_target="tpu_custom_call" | custom-call | flops 8280000000 | tf_op jit(solution)/shard_map/attention/pallas_call | solution.py:78
  40.8 5.0 %attention.3 = (bf16[1024,512]{1,0:T(8,128)(2,1)S(1)}, bf16[1024,1536]{1,0:T(8,128)(2,1)S(1)}, bf16[1024,512]{1,0:T(8,128)(2,1)S(1)}, f32[4,4,512]{2,1,0:T(4,128)S(1)}) custom-call(s32[1]{0:T(128)} %bitcast.refs_0_, s32[4]{0:T(128)S(1)} %copy-done.18, s32[4]{0:T(128)S(1)} %copy-done.17, s32[4,1,256]{2,1,0:T(1,128)S(1)} %reshape.50.refs_3_.refs_2_, ...), custom_call_target="tpu_custom_call" | custom-call | flops 8280000000 | tf_op jit(solution)/shard_map/attention/pallas_call | solution.py:78
  45.8 6.1 %collective-permute-done.13.refs_8_.refs_5_ = bf16[128,2560]{1,0:T(8,128)(2,1)S(1)} collective-permute-done((bf16[128,2560]{1,0:T(8,128)(2,1)S(1)}, bf16[128,2560]{1,0:T(8,128)(2,1)S(1)}, u32[]{:S(2)}, u32[]{:S(2)}) %collective-permute-start.13) | collective-permute-done | bytes 655392 | tf_op jit(solution)/shard_map/ppermute | solution.py:590
  54.0 6.9 %hidden0.1 = (f32[1024,512]{1,0:T(8,128)S(1)}, bf16[1024,512]{1,0:T(8,128)(2,1)S(1)}, f32[1024,512]{1,0:T(8,128)S(1)}, bf16[512,512]{1,0:T(8,128)(2,1)S(1)}, bf1...) custom-call(s32[1]{0:T(128)} %bitcast.refs_0_, ...), custom_call_target="tpu_custom_call" | custom-call | flops 11729999872 | tf_op jit(solution)/shard_map/hidden0/pallas_call | solution.py:78
  61.7 4.3 %hidden1.1 = (f32[1024,512]{1,0:T(8,128)S(1)}, bf16[1024,512]{1,0:T(8,128)(2,1)S(1)}, bf16[512,512]{1,0:T(8,128)(2,1)S(1)}, f32[256,2048]{1,0:T(8,128)S(1)}, bf16[256,2048]{1,0:T(8,128)(2,1)S(1)}) custom-call(s32[1]{0:T(128)} %bitcast.refs_0_, bf16[1024,512]{1,0:T(8,128)(2,1)S(1)} %bitcast.6, ...), custom_call_target="tpu_custom_call", output_to_operand_aliasing={{0}: (3, {})} | custom-call | flops 8970000384 | tf_op jit(solution)/shard_map/hidden1/pallas_call | solution.py:78
  66.6 4.1 %hidden2.1 = (f32[1024,512]{1,0:T(8,128)S(1)}, bf16[1024,512]{1,0:T(8,128)(2,1)S(1)}, bf16[512,512]{1,0:T(8,128)(2,1)S(1)}, f32[512,512]{1,0:T(8,128)S(1)}, f32[512,512]{1,0:T(8,128)S(1)}) custom-call(s32[1]{0:T(128)} %bitcast.refs_0_, bf16[1024,512]{1,0:T(8,128)(2,1)S(1)} %bitcast.7, ...), custom_call_target="tpu_custom_call", output_to_operand_aliasing={{0}: (3, {})} | custom-call | flops 8970000384 | tf_op jit(solution)/shard_map/hidden2/pallas_call | solution.py:78
  72.5 4.1 %hidden3.1 = (f32[1024,512]{1,0:T(8,128)S(1)}, bf16[1024,512]{1,0:T(8,128)(2,1)S(1)}, bf16[512,512]{1,0:T(8,128)(2,1)S(1)}, f32[512,512]{1,0:T(8,128)S(1)}, f32[512,512]{1,0:T(8,128)S(1)}) custom-call(s32[1]{0:T(128)} %bitcast.refs_0_, bf16[1024,512]{1,0:T(8,128)(2,1)S(1)} %bitcast.8, ...), custom_call_target="tpu_custom_call", output_to_operand_aliasing={{0}: (3, {})} | custom-call | flops 8970000384 | tf_op jit(solution)/shard_map/hidden3/pallas_call | solution.py:78
  76.7 3.3 %middle_back.1 = (f32[1024,512]{1,0:T(8,128)S(1)}, bf16[1024,512]{1,0:T(8,128)(2,1)S(1)}, f32[8,512]{1,0:T(8,128)S(1)}, f32[256,2560]{1,0:T(8,128)S(1)}, bf16[256,2560]{1,0:T(8,128)(2,1)S(1)}) custom-call(s32[1]{0:T(128)} %bitcast.refs_0_, bf16[1024,512]{1,0:T(8,128)(2,1)S(1)} %bitcast.9, f32[8,512]{1,0:T(8,128)S(1)} %get-tuple-element.150.refs_6_.refs_5_.refs_2_.refs_4_, ...), custom_call_target="tpu_custom_call" | custom-call | flops 5520000000 | tf_op jit(solution)/shard_map/middle_back/pallas_call | solution.py:78
  81.1 3.8 %attention_back.4 = (bf16[1024,384]{1,0:T(8,128)(2,1)S(1)}, f32[512,384]{1,0:T(8,128)S(1)}) custom-call(s32[1]{0:T(128)} %bitcast.refs_0_, s32[4]{0:T(128)S(1)} %copy-done.17, bf16[1024,512]{1,0:T(8,128)(2,1)S(1)} %get-tuple-element.160.refs_2_.refs_6_, bf16[1024,1536]{1,0:T(8,128)(2,1)S(1)} %get-tuple-element.161.refs_3_, ...), custom_call_target="tpu_custom_call" | custom-call | flops 6347999744 | tf_op jit(solution)/shard_map/attention_back/pallas_call | solution.py:78
  86.9 2.7 %collective-permute-start.27 = (bf16[16,2048]{1,0:T(8,128)(2,1)S(1)}, bf16[16,2048]{1,0:T(8,128)(2,1)S(1)}, u32[]{:S(2)}, u32[]{:S(2)}) collective-permute-start(bf16[16,2048]{1,0:T(8,128)(2,1)S(1)} %get-tuple-element.266), channel_id=1, source_target_pairs={{0,24},{1,25},{2,26},{3,27},{4,28},{5,29},{6,30},{7,31},{8,16},{9,... | collective-permute-start | bytes 196616 | tf_op jit(solution)/shard_map/ppermute | solution.py:590
  93.2 3.6 %attention_back.6 = (bf16[1024,384]{1,0:T(8,128)(2,1)S(1)}, f32[256,768]{1,0:T(8,128)S(1)}, bf16[256,768]{1,0:T(8,128)(2,1)S(1)}) custom-call(s32[1]{0:T(128)} %bitcast.refs_0_, s32[4]{0:T(128)S(1)} %copy-done.17, bf16[1024,512]{1,0:T(8,128)(2,1)S(1)} %get-tuple-element.160.refs_2_.refs_6_, bf16[1024,1536]{1,0:T(8,128)(2,1)S(1)} %get-tuple-element.161.refs_3_, ...), custom_call_target="tpu_custom_call" | custom-call | flops 6347999744 | tf_op jit(solution)/shard_map/attention_back/pallas_call | solution.py:78
  96.9 3.6 %attention_back.5 = (bf16[1024,384]{1,0:T(8,128)(2,1)S(1)}, f32[512,384]{1,0:T(8,128)S(1)}) custom-call(s32[1]{0:T(128)} %bitcast.refs_0_, s32[4]{0:T(128)S(1)} %copy-done.17, bf16[1024,512]{1,0:T(8,128)(2,1)S(1)} %get-tuple-element.160.refs_2_.refs_6_, bf16[1024,1536]{1,0:T(8,128)(2,1)S(1)} %get-tuple-element.161.refs_3_, ...), custom_call_target="tpu_custom_call" | custom-call | flops 6347999744 | tf_op jit(solution)/shard_map/attention_back/pallas_call | solution.py:78
  102.4 2.8 %attention_back.7.refs_12_ = bf16[1024,384]{1,0:T(8,128)(2,1)S(1)} custom-call(s32[1]{0:T(128)} %bitcast.refs_0_, s32[4]{0:T(128)S(1)} %copy-done.17, bf16[1024,512]{1,0:T(8,128)(2,1)S(1)} %get-tuple-element.160.refs_2_.refs_6_, bf16[1024,1536]{1,0:T(8,128)(2,1)S(1)} %get-tuple-element.161.refs_3_, f32[4,4,512]{2,1,0:T(4,128)S(1)} %get-tuple-element.154.refs_4_, ...), custom_call_target="tpu_custom_call" | custom-call | flops 6347999744 | tf_op jit(solution)/shard_map/attention_back/pallas_call | solution.py:78
  107.2 6.0 %input_back.1 = (f32[1024,512]{1,0:T(8,128)}, f32[256,896]{1,0:T(8,128)S(1)}, bf16[256,896]{1,0:T(8,128)(2,1)S(1)}) custom-call(s32[1]{0:T(128)} %bitcast.refs_0_, s32[4]{0:T(128)S(1)} %copy-done.18, s32[4,1,256]{2,1,0:T(1,128)S(1)} %reshape.50.refs_3_.refs_2_, bf16[1024,512]{1,0:T(8,128)(2,1)S(1)} %bitcast.13, ...), custom_call_target="tpu_custom_call" | custom-call | flops 8970000384 | tf_op jit(solution)/shard_map/input_back/pallas_call | solution.py:78
  114.7 2.7 %collective-permute-start.33 = (bf16[16,3328]{1,0:T(8,128)(2,1)S(1)}, bf16[16,3328]{1,0:T(8,128)(2,1)S(1)}, u32[]{:S(2)}, u32[]{:S(2)}) collective-permute-start(bf16[16,3328]{1,0:T(8,128)(2,1)S(1)} %get-tuple-element.263), channel_id=1, source_target_pairs={{0,24},{1,25},{2,26},{3,27},{4,28},{5,29},{6,30},{7,31},{8,16},{9,... | collective-permute-start | bytes 319496 | tf_op jit(solution)/shard_map/ppermute | solution.py:590
  123.4 2.6 %collective-permute-done.32.refs_2_.refs_6_ = bf16[16,3328]{1,0:T(8,128)(2,1)S(1)} collective-permute-done((bf16[16,3328]{1,0:T(8,128)(2,1)S(1)}, bf16[16,3328]{1,0:T(8,128)(2,1)S(1)}, u32[]{:S(2)}, u32[]{:S(2)}) %collective-permute-start.32) | collective-permute-done | bytes 106528 | tf_op jit(solution)/shard_map/ppermute | solution.py:590
  127.5 4.1 %collective-permute-done.35 = bf16[64,896]{1,0:T(8,128)(2,1)S(1)} collective-permute-done((bf16[64,896]{1,0:T(8,128)(2,1)S(1)}, bf16[64,896]{1,0:T(8,128)(2,1)S(1)}, u32[]{:S(2)}, u32[]{:S(2)}) %collective-permute-start.35) | collective-permute-done | bytes 114720 | tf_op jit(solution)/shard_map/ppermute | solution.py:590
  131.6 2.7 %collective-permute-start.38 = (bf16[16,896]{1,0:T(8,128)(2,1)S(1)}, bf16[16,896]{1,0:T(8,128)(2,1)S(1)}, u32[]{:S(2)}, u32[]{:S(2)}) collective-permute-start(bf16[16,896]{1,0:T(8,128)(2,1)S(1)} %get-tuple-element.273), channel_id=1, source_target_pairs={{0,24},{1,25},{2,26},{3,27},{4,28},{5,29},{6,30},{7,31},{8,16},{9,... | collective-permute-start | bytes 86024 | tf_op jit(solution)/shard_map/ppermute | solution.py:590
  136.2 2.7 %hidden_update.1 = (f32[16,2048]{1,0:T(8,128)}, f32[16,2048]{1,0:T(8,128)}, f32[16,2048]{1,0:T(8,128)}, f32[64,512]{1,0:T(8,128)}, f32[64,512]{1,0:T(8,128)}, /*...) custom-call(f32[64,2048]{1,0:T(8,128)S(1)} %get-tuple-element.244.refs_0_, ...), custom_call_target="tpu_custom_call" | custom-call | flops 4140000000 | tf_op jit(solution)/shard_map/hidden_update/pallas_call | solution.py:536
  (154 shorter events, 42.8 us)
Async XLA Ops:
  2.2 7.4 %collective-permute-start.2 = (bf16[16,1664]{1,0:T(8,128)(2,1)S(1)}, bf16[16,1664]{1,0:T(8,128)(2,1)S(1)}, u32[]{:S(2)}, u32[]{:S(2)}) collective-permute-start(bf16[16,1664]{1,0:T(8,128)(2,1)S(1)} %get-tuple-element.138), channel_id=1, source_target_pairs={{0,24},{1,25},{2,26},{3,27},{4,28},{5,29},{6,30},{7,31},{8,16},{9,... | collective-permute-start | bytes 159752 | tf_op jit(solution)/shard_map/ppermute | solution.py:590
  12.4 7.4 %collective-permute-start.5 = (bf16[64,1664]{1,0:T(8,128)(2,1)S(1)}, bf16[64,1664]{1,0:T(8,128)(2,1)S(1)}, u32[]{:S(2)}, u32[]{:S(2)}) collective-permute-start(bf16[64,1664]{1,0:T(8,128)(2,1)S(1)} %pad_maximum_fusion.4), channel_id=1, source_target_pairs={{0,4},{1,3},{2,6},{3,1},{4,0},{5,7},{6,2},{7,5},{8,12},{9,11},{10,... | collective-permute-start | bytes 638984 | tf_op jit(solution)/shard_map/ppermute | solution.py:590
  15.4 8.6 %collective-permute-start.10 = (bf16[16,4608]{1,0:T(8,128)(2,1)S(1)}, bf16[16,4608]{1,0:T(8,128)(2,1)S(1)}, u32[]{:S(2)}, u32[]{:S(2)}) collective-permute-start(bf16[16,4608]{1,0:T(8,128)(2,1)S(1)} %get-tuple-element.139), channel_id=1, source_target_pairs={{0,24},{1,25},{2,26},{3,27},{4,28},{5,29},{6,30},{7,31},{8,16},{9,... | collective-permute-start | bytes 442376 | tf_op jit(solution)/shard_map/ppermute | solution.py:590
  17.8 13.3 %collective-permute-start.9 = (bf16[16,4608]{1,0:T(8,128)(2,1)S(1)}, bf16[16,4608]{1,0:T(8,128)(2,1)S(1)}, u32[]{:S(2)}, u32[]{:S(2)}) collective-permute-start(bf16[16,4608]{1,0:T(8,128)(2,1)S(1)} %get-tuple-element.139), channel_id=1, source_target_pairs={{0,16},{1,17},{2,18},{3,19},{4,20},{5,21},{6,22},{7,23},{8,24},{9,... | collective-permute-start | bytes 442376 | tf_op jit(solution)/shard_map/ppermute | solution.py:590
  17.8 13.3 %collective-permute-start.4 = (bf16[16,4608]{1,0:T(8,128)(2,1)S(1)}, bf16[16,4608]{1,0:T(8,128)(2,1)S(1)}, u32[]{:S(2)}, u32[]{:S(2)}) collective-permute-start(bf16[16,4608]{1,0:T(8,128)(2,1)S(1)} %get-tuple-element.139), channel_id=1, source_target_pairs={{0,8},{1,9},{2,10},{3,11},{4,12},{5,13},{6,14},{7,15},{8,0},{9,1},... | collective-permute-start | bytes 442376 | tf_op jit(solution)/shard_map/ppermute | solution.py:590
  19.8 11.3 %collective-permute-start.7 = (bf16[64,1664]{1,0:T(8,128)(2,1)S(1)}, bf16[64,1664]{1,0:T(8,128)(2,1)S(1)}, u32[]{:S(2)}, u32[]{:S(2)}) collective-permute-start(bf16[64,1664]{1,0:T(8,128)(2,1)S(1)} %collective-permute-done.5), channel_id=1, source_target_pairs={{0,1},{1,0},{2,3},{3,2},{4,5},{5,4},{6,7},{7,6},{8,9},{9,8},{10,11... | collective-permute-start | bytes 638984 | tf_op jit(solution)/shard_map/ppermute | solution.py:590
  19.9 11.3 %collective-permute-start.6 = (bf16[128,1664]{1,0:T(8,128)(2,1)S(1)}, bf16[128,1664]{1,0:T(8,128)(2,1)S(1)}, u32[]{:S(2)}, u32[]{:S(2)}) collective-permute-start(bf16[128,1664]{1,0:T(8,128)(2,1)S(1)} %constant_dynamic-update-slice_fusion.refs_5_), channel_id=1, source_target_pairs={{0,2},{1,5},{2,0},{3,7},{4,6},{5,1},{6,4},{7,3},{8,10},{9,13},{10,... | collective-permute-start | bytes 1277960 | tf_op jit(solution)/shard_map/ppermute | solution.py:590
  38.5 15.5 %collective-permute-start.14 = (bf16[128,2560]{1,0:T(8,128)(2,1)S(1)}, bf16[128,2560]{1,0:T(8,128)(2,1)S(1)}, u32[]{:S(2)}, u32[]{:S(2)}) collective-permute-start(bf16[128,2560]{1,0:T(8,128)(2,1)S(1)} %constant_dynamic-update-slice_fusion.5.refs_7_.refs_4_), channel_id=1, source_target_pairs={{0,1},{1,0},{2,3},{3,2},{4,5},{5,4},{6,7},{7,6},{8,9},{9,8},{10,11... | collective-permute-start | bytes 1966088 | tf_op jit(solution)/shard_map/ppermute | solution.py:590
  38.6 13.3 %collective-permute-start.13 = (bf16[128,2560]{1,0:T(8,128)(2,1)S(1)}, bf16[128,2560]{1,0:T(8,128)(2,1)S(1)}, u32[]{:S(2)}, u32[]{:S(2)}) collective-permute-start(bf16[128,2560]{1,0:T(8,128)(2,1)S(1)} %constant_dynamic-update-slice_fusion.5.refs_7_.refs_4_), channel_id=1, source_target_pairs={{0,2},{1,5},{2,0},{3,7},{4,6},{5,1},{6,4},{7,3},{8,10},{9,13},{10,... | collective-permute-start | bytes 1966088 | tf_op jit(solution)/shard_map/ppermute | solution.py:590
  40.2 11.7 %collective-permute-start.11 = (bf16[64,2048]{1,0:T(8,128)(2,1)S(1)}, bf16[64,2048]{1,0:T(8,128)(2,1)S(1)}, u32[]{:S(2)}, u32[]{:S(2)}) collective-permute-start(bf16[64,2048]{1,0:T(8,128)(2,1)S(1)} %pad_maximum_fusion.3), channel_id=1, source_target_pairs={{0,4},{1,3},{2,6},{3,1},{4,0},{5,7},{6,2},{7,5},{8,12},{9,11},{10,... | collective-permute-start | bytes 786440 | tf_op jit(solution)/shard_map/ppermute | solution.py:590
  51.9 9.0 %collective-permute-start.18 = (bf16[128,2048]{1,0:T(8,128)(2,1)S(1)}, bf16[128,2048]{1,0:T(8,128)(2,1)S(1)}, u32[]{:S(2)}, u32[]{:S(2)}) collective-permute-start(bf16[128,2048]{1,0:T(8,128)(2,1)S(1)} %constant_dynamic-update-slice_fusion.10.refs_4_), channel_id=1, source_target_pairs={{0,1},{1,0},{2,3},{3,2},{4,5},{5,4},{6,7},{7,6},{8,9},{9,8},{10,11... | collective-permute-start | bytes 1572872 | tf_op jit(solution)/shard_map/ppermute | solution.py:590
  52.5 9.2 %collective-permute-start.17 = (bf16[128,2048]{1,0:T(8,128)(2,1)S(1)}, bf16[128,2048]{1,0:T(8,128)(2,1)S(1)}, u32[]{:S(2)}, u32[]{:S(2)}) collective-permute-start(bf16[128,2048]{1,0:T(8,128)(2,1)S(1)} %constant_dynamic-update-slice_fusion.10.refs_4_), channel_id=1, source_target_pairs={{0,2},{1,5},{2,0},{3,7},{4,6},{5,1},{6,4},{7,3},{8,10},{9,13},{10,... | collective-permute-start | bytes 1572872 | tf_op jit(solution)/shard_map/ppermute | solution.py:590
  71.0 9.2 %collective-permute-start.21 = (bf16[128,2048]{1,0:T(8,128)(2,1)S(1)}, bf16[128,2048]{1,0:T(8,128)(2,1)S(1)}, u32[]{:S(2)}, u32[]{:S(2)}) collective-permute-start(bf16[128,2048]{1,0:T(8,128)(2,1)S(1)} %get-tuple-element.175), channel_id=1, source_target_pairs={{0,2},{1,5},{2,0},{3,7},{4,6},{5,1},{6,4},{7,3},{8,10},{9,13},{10,... | collective-permute-start | bytes 1572872 | tf_op jit(solution)/shard_map/ppermute | solution.py:590
  80.0 11.4 %collective-permute-start.20 = (bf16[256,2560]{1,0:T(8,128)(2,1)S(1)}, bf16[256,2560]{1,0:T(8,128)(2,1)S(1)}, u32[]{:S(2)}, u32[]{:S(2)}) collective-permute-start(bf16[256,2560]{1,0:T(8,128)(2,1)S(1)} %get-tuple-element.186), channel_id=1, source_target_pairs={{0,1},{1,0},{2,3},{3,2},{4,5},{5,4},{6,7},{7,6},{8,9},{9,8},{10,11... | collective-permute-start | bytes 3932168 | tf_op jit(solution)/shard_map/ppermute | solution.py:590
  86.9 13.6 %collective-permute-start.27 = (bf16[16,2048]{1,0:T(8,128)(2,1)S(1)}, bf16[16,2048]{1,0:T(8,128)(2,1)S(1)}, u32[]{:S(2)}, u32[]{:S(2)}) collective-permute-start(bf16[16,2048]{1,0:T(8,128)(2,1)S(1)} %get-tuple-element.266), channel_id=1, source_target_pairs={{0,24},{1,25},{2,26},{3,27},{4,28},{5,29},{6,30},{7,31},{8,16},{9,... | collective-permute-start | bytes 196616 | tf_op jit(solution)/shard_map/ppermute | solution.py:590
  89.6 10.9 %collective-permute-start.26 = (bf16[16,2048]{1,0:T(8,128)(2,1)S(1)}, bf16[16,2048]{1,0:T(8,128)(2,1)S(1)}, u32[]{:S(2)}, u32[]{:S(2)}) collective-permute-start(bf16[16,2048]{1,0:T(8,128)(2,1)S(1)} %get-tuple-element.267), channel_id=1, source_target_pairs={{0,16},{1,17},{2,18},{3,19},{4,20},{5,21},{6,22},{7,23},{8,24},{9,... | collective-permute-start | bytes 196616 | tf_op jit(solution)/shard_map/ppermute | solution.py:590
  89.6 10.9 %collective-permute-start.25 = (bf16[16,2048]{1,0:T(8,128)(2,1)S(1)}, bf16[16,2048]{1,0:T(8,128)(2,1)S(1)}, u32[]{:S(2)}, u32[]{:S(2)}) collective-permute-start(bf16[16,2048]{1,0:T(8,128)(2,1)S(1)} %get-tuple-element.268), channel_id=1, source_target_pairs={{0,8},{1,9},{2,10},{3,11},{4,12},{5,13},{6,14},{7,15},{8,0},{9,1},... | collective-permute-start | bytes 196616 | tf_op jit(solution)/shard_map/ppermute | solution.py:590
  91.6 10.7 %collective-permute-start.22 = (bf16[128,2560]{1,0:T(8,128)(2,1)S(1)}, bf16[128,2560]{1,0:T(8,128)(2,1)S(1)}, u32[]{:S(2)}, u32[]{:S(2)}) collective-permute-start(bf16[128,2560]{1,0:T(8,128)(2,1)S(1)} %get-tuple-element.193), channel_id=1, source_target_pairs={{0,2},{1,5},{2,0},{3,7},{4,6},{5,1},{6,4},{7,3},{8,10},{9,13},{10,... | collective-permute-start | bytes 1966088 | tf_op jit(solution)/shard_map/ppermute | solution.py:590
  106.4 8.2 %collective-permute-start.30 = (bf16[64,3328]{1,0:T(8,128)(2,1)S(1)}, bf16[64,3328]{1,0:T(8,128)(2,1)S(1)}, u32[]{:S(2)}, u32[]{:S(2)}) collective-permute-start(bf16[64,3328]{1,0:T(8,128)(2,1)S(1)} %pad_maximum_fusion.1), channel_id=1, source_target_pairs={{0,4},{1,3},{2,6},{3,1},{4,0},{5,7},{6,2},{7,5},{8,12},{9,11},{10,... | collective-permute-start | bytes 1277960 | tf_op jit(solution)/shard_map/ppermute | solution.py:590
  113.2 7.2 %collective-permute-start.29 = (bf16[256,896]{1,0:T(8,128)(2,1)S(1)}, bf16[256,896]{1,0:T(8,128)(2,1)S(1)}, u32[]{:S(2)}, u32[]{:S(2)}) collective-permute-start(bf16[256,896]{1,0:T(8,128)(2,1)S(1)} %get-tuple-element.219), channel_id=1, source_target_pairs={{0,1},{1,0},{2,3},{3,2},{4,5},{5,4},{6,7},{7,6},{8,9},{9,8},{10,11... | collective-permute-start | bytes 1376264 | tf_op jit(solution)/shard_map/ppermute | solution.py:590
  114.7 8.7 %collective-permute-start.33 = (bf16[16,3328]{1,0:T(8,128)(2,1)S(1)}, bf16[16,3328]{1,0:T(8,128)(2,1)S(1)}, u32[]{:S(2)}, u32[]{:S(2)}) collective-permute-start(bf16[16,3328]{1,0:T(8,128)(2,1)S(1)} %get-tuple-element.263), channel_id=1, source_target_pairs={{0,24},{1,25},{2,26},{3,27},{4,28},{5,29},{6,30},{7,31},{8,16},{9,... | collective-permute-start | bytes 319496 | tf_op jit(solution)/shard_map/ppermute | solution.py:590
  117.4 8.6 %collective-permute-start.32 = (bf16[16,3328]{1,0:T(8,128)(2,1)S(1)}, bf16[16,3328]{1,0:T(8,128)(2,1)S(1)}, u32[]{:S(2)}, u32[]{:S(2)}) collective-permute-start(bf16[16,3328]{1,0:T(8,128)(2,1)S(1)} %get-tuple-element.264), channel_id=1, source_target_pairs={{0,16},{1,17},{2,18},{3,19},{4,20},{5,21},{6,22},{7,23},{8,24},{9,... | collective-permute-start | bytes 319496 | tf_op jit(solution)/shard_map/ppermute | solution.py:590
  117.4 8.6 %collective-permute-start.31 = (bf16[16,3328]{1,0:T(8,128)(2,1)S(1)}, bf16[16,3328]{1,0:T(8,128)(2,1)S(1)}, u32[]{:S(2)}, u32[]{:S(2)}) collective-permute-start(bf16[16,3328]{1,0:T(8,128)(2,1)S(1)} %get-tuple-element.265), channel_id=1, source_target_pairs={{0,8},{1,9},{2,10},{3,11},{4,12},{5,13},{6,14},{7,15},{8,0},{9,1},... | collective-permute-start | bytes 319496 | tf_op jit(solution)/shard_map/ppermute | solution.py:590
  131.6 7.3 %collective-permute-start.38 = (bf16[16,896]{1,0:T(8,128)(2,1)S(1)}, bf16[16,896]{1,0:T(8,128)(2,1)S(1)}, u32[]{:S(2)}, u32[]{:S(2)}) collective-permute-start(bf16[16,896]{1,0:T(8,128)(2,1)S(1)} %get-tuple-element.273), channel_id=1, source_target_pairs={{0,24},{1,25},{2,26},{3,27},{4,28},{5,29},{6,30},{7,31},{8,16},{9,... | collective-permute-start | bytes 86024 | tf_op jit(solution)/shard_map/ppermute | solution.py:590
  (35 other events, 295.0 us)
where the time goes:
time: 140 us
  Pallas kernels  62.1 us (44%)
  starting transfers between devices  39.2 us (28%)
  waiting for transfers between devices  36.6 us (26%)
    pallas_call x14, Pallas kernels, call(): pl.pallas_call(kernel, out_shape=[jax.ShapeDtypeStruct(shape, kind) for _...  56 us
    ppermute x39, starting transfers between devices, exchange(): return lax.ppermute(values, AXES, pairs)  39.2 us
    ppermute x39, waiting for transfers between devices, exchange(): return lax.ppermute(values, AXES, pairs)  36.6 us
  transfers between devices with their start and end apart: 39, of which 18 were waited for; matrix products, arithmetic and copies ran while one was open for 0% of the time, Pallas kernels for 43%

commit v1 on v0

--- a/solution.py
+++ b/solution.py
@@ -18,7 +18,9 @@
 STEP = 10
 AXES = ("dp", "fsdp")
 SCALE = 1.2
-NEAR_PARTS = 3
+FIRST_HALF = 4 * QUARTER + D + 6 * LANES
+REAR_COST = 0.5
+IN_VMEM = ("input_grad",)
 UNROLL = 2
 VMEM_BYTES = 16 * 1024 * 1024
 
@@ -77,10 +79,12 @@
 
     results = pl.pallas_call(
         kernel,
-        out_shape=[jax.ShapeDtypeStruct(shape, kind) for _, shape, kind in outs],
+        out_shape=[(pltpu.VMEM if entry in IN_VMEM and len(_) == 0 else jax.ShapeDtypeStruct)(shape, kind) for entry, shape, kind, *_ in outs],
         in_specs=[entry[2] if len(entry) > 2 else whole() for entry in ins],
-        out_specs=[whole() for _ in outs],
-        scratch_shapes=[pltpu.VMEM(shape, kind) for _, shape, kind in scratch],
+        out_specs=[whole() if len(entry) == 3 else pl.BlockSpec(memory_space=pl.ANY) for entry in outs],
+        scratch_shapes=[
+            pltpu.SemaphoreType.DMA(shape) if kind is None else pltpu.VMEM(shape, kind) for _, shape, kind in scratch
+        ],
         compiler_params=pltpu.CompilerParams(vmem_limit_bytes=VMEM_BYTES),
         cost_estimate=cost(micros),
         input_output_aliases=aliases,
@@ -241,7 +245,7 @@
     else:
         ins += [("weight", front.weight), ("vec", front.vec)]
         ins += [("front_" + name, getattr(front, name)) for name in ("normed", "p", "attended", "logs")]
-    return call(body, "attention", 3 * len(spans), ins, outs, scratch)
+    return call(body, "attention", 6 if fresh else REAR_COST, ins, outs, scratch)
 
 
 def hidden_quarter(normed, upstream, up, down):
@@ -360,25 +364,45 @@
     return call(body, "middle_back", 4, ins, outs, scratch)
 
 
-def branch_output(middle, quarters, seq, spans, front=None):
+def branch_output(middle, quarters, seq, spans, front=None, grad=None):
+    rows_before = spans[0] * seq
+    rows_here = len(spans) * seq
+
     def body(r):
+        copies = []
         if front is not None:
-            r.result[pl.ds(0, front.shape[0]), :] = r.front[...]
+            here = pl.ds(rows_before, rows_here)
+            copies = [
+                pltpu.make_async_copy(r.grad, r.input_grad, r.done.at[0]),
+                pltpu.make_async_copy(r.front, r.result.at[pl.ds(0, rows_before), :], r.done.at[1]),
+                pltpu.make_async_copy(r.rear, r.result.at[here, :], r.done.at[2]),
+            ]
+            copies[0].start()
+            copies[1].start()
+        target = r.result if front is None else r.rear
 
         def one_span(span, rows):
             result = r.middle[rows, :]
             for n in range(4):
                 result = result + dot(getattr(r, "active%d" % n)[rows, :], getattr(r, "down%d" % n)[...])
-            r.result[rows, :] = low(result)
+            target[pl.ds(pl.multiple_of((span - spans[0]) * seq, seq), seq), :] = low(result)
 
         each_span(seq, spans, one_span)
+        if front is not None:
+            copies[2].start()
+            for copy in copies:
+                copy.wait()
 
     ins = [("middle", middle)]
     for n, quarter in enumerate(quarters):
         ins += [("active%d" % n, quarter.active), ("down%d" % n, quarter.down_full)]
-    if front is not None:
-        ins += [("front", front)]
-    return call(body, "branch_output", 25, ins, [("result", ((spans[-1] + 1) * seq, D), jnp.bfloat16)]).result
+    if front is None:
+        return call(body, "branch_output", 25, ins, [("result", (rows_here, D), jnp.bfloat16)]).result
+    ins += [("front", front), ("grad", grad)]
+    outs = [("result", (rows_before + rows_here, D), jnp.bfloat16, True), ("input_grad", grad.shape, jnp.float32, True)]
+    scratch = [("rear", (rows_here, D), jnp.bfloat16), ("done", (3,), None)]
+    done = call(body, "branch_output", 25, ins, outs, scratch)
+    return done.result, done.input_grad
 
 
 def attention_back(scalar, pair, normed, p, logs, dattended, seq, mate=None):
@@ -500,12 +524,16 @@
 
 
 def hidden_update_kernel(*refs):
-    halves = (refs[0:4], refs[4:8])
-    up, down, out = refs[8:11], refs[11:14], refs[14:17]
-    new_up, new_down, new_out = refs[17:20], refs[20:23], refs[23:26]
-
-    def summed(half, columns):
-        return half[0][:ROWS, columns] + sum(wide(part[:, columns]) for part in half[1:])
+    total, parts = refs[0], refs[1:4]
+    up, down, out = refs[4:7], refs[7:10], refs[10:13]
+    new_up, new_down, new_out = refs[13:16], refs[16:19], refs[19:22]
+
+    def summed(column, width):
+        columns = pl.ds(column, width)
+        return total[:ROWS, columns] + sum(wide(part[:, columns]) for part in parts)
+
+    def start(quarter):
+        return FIRST_HALF * (1 - quarter // 2) + (quarter % 2) * 2 * QUARTER
 
     def update(new, old, index, grad, rate):
         results = adam_update(old[0][index], grad, old[1][index], old[2][index], rate, weight_decay)
@@ -516,8 +544,7 @@
     for group in range(FF // D):
         grads = []
         for quarter in range(4):
-            columns = pl.ds((quarter % 2) * 2 * QUARTER + group * LANES, LANES)
-            grads.append(summed(halves[quarter // 2], columns))
+            grads.append(summed(start(quarter) + group * LANES, LANES))
         rest = jnp.concatenate(grads, axis=1)
         grad = 0.0
         for _ in range(3):
@@ -526,22 +553,22 @@
             rest = rest - wide(piece)
         update(new_up, up, (slice(None), pl.ds(group * D, D)), grad, matrix_rate)
     for quarter in range(4):
-        grad = summed(halves[quarter // 2], pl.ds((quarter % 2) * 2 * QUARTER + QUARTER, D))
+        grad = summed(start(quarter) + QUARTER, D)
         update(new_down, down, (pl.ds(quarter * ROWS, ROWS), slice(None)), grad, matrix_rate)
-    update(new_out, out, Ellipsis, summed(halves[1], pl.ds(4 * QUARTER, D)), output_rate)
-
-
-def hidden_update(total_one, parts_one, total_two, parts_two, up, down, out):
+    update(new_out, out, Ellipsis, summed(4 * QUARTER, D), output_rate)
+
+
+def hidden_update(total, parts, up, down, out):
     outs = [jax.ShapeDtypeStruct(state[0].shape, jnp.float32) for state in (up, down, out) for _ in range(3)]
     results = pl.pallas_call(
         hidden_update_kernel,
         out_shape=outs,
-        in_specs=[whole()] * 17,
+        in_specs=[whole()] * 13,
         out_specs=[whole()] * 9,
         compiler_params=pltpu.CompilerParams(vmem_limit_bytes=VMEM_BYTES),
         cost_estimate=cost(3),
         name="hidden_update",
-    )(total_one, *parts_one, total_two, *parts_two, *up, *down, *out)
+    )(total, *parts, *up, *down, *out)
     return results[:3], results[3:6], results[6:]
 
 
@@ -805,15 +832,16 @@
     one = Gather(piece_one, count)
     one.far()
     one.stack()
-    rest = Gather(tie(piece_rest, one.core()), count)
-    three, two = rest.split(4 * QUARTER)
+    two = Gather(tie(piece_rest[:, 4 * QUARTER :], one.core()), count)
+    two.far()
     one.near()
     one.late()
-    one.core()
+    three = Gather(tie(piece_rest[:, : 4 * QUARTER], one.core()), count)
+    three.far()
     first = one.finish()
-    two.stack(*([one.rest] if direct else []))
+    two.stack()
     front = attention(scalar, order, flat, first, range(0, spans // 2))
-    two.near(front.logs)
+    two.near()
     two.late()
     two.core()
     three.stack(front.logs)
@@ -845,33 +873,34 @@
     parts += [part(1, sum_one.next(parts[0].dp), *sum_two.core(parts[0].dp), mate=parts[0])]
     early = Scatter(parts[1], count, direct)
     parts += [part(2, sum_one.total)]
-    parts_one = sum_one.parts(parts[2].dp)
     early.core(parts[2].dp)
     sum_two.near(parts[2].dp)
-    parts += [part(3, sum_two.total, early.total, *parts_one)]
+    parts += [part(3, sum_two.total, early.total)]
     early.near(parts[3].dp)
     if direct:
         sum_two.join(early)
     ready = tie(flat, parts[3].dp, sum_two.total)
     final = input_back(scalar, order, ready, vec, rear.normed, turn.dmiddle, weight, turn.dvec, parts)
     late = Scatter(final, count, direct)
-    sum_two.next(final.input_grad)
-    result = branch_output(tie(h[0].middle, sum_two.total), h, seq, range(0, spans // 2))
+    result = branch_output(tie(h[0].middle, final.input_grad), h, seq, range(0, spans // 2))
+    sum_two.next(result)
     late.core(result)
-    result = branch_output(tie(h[0].middle, late.total), h, seq, range(spans // 2, spans), result)
-    parts_two = sum_two.parts() if direct else []
-    late.near(result, *parts_two[:NEAR_PARTS])
+    middle = tie(h[0].middle, late.total)
+    result, input_grad = branch_output(middle, h, seq, range(spans // 2, spans), result, final.input_grad)
+    if direct:
+        sum_two.total = jnp.concatenate([sum_two.total, sum_one.total], axis=1)
+    parts_two = sum_two.parts()
+    late.near(result)
     qkv_state = (weight_qkv, moment_qkv, square_qkv)
     vec_state = (vectors, moment_vec, square_vec)
     out_state = (weight_out, moment_out, square_out)
     up_state = (weight_up, moment_up, square_up)
     down_state = (weight_down, moment_down, square_down)
     if direct:
-        late.next(*parts_two)
+        states = hidden_update(tie(sum_two.total, late.send), parts_two, up_state, down_state, out_state)
+        new_up, new_down, new_out = states
+        late.next()
         parts_late = late.parts()
-        total_one = tie(sum_one.total, late.total)
-        states = hidden_update(total_one, parts_one, sum_two.total, parts_two, up_state, down_state, out_state)
-        new_up, new_down, new_out = states
         new_qkv, new_vec = last_update(sum_two.total, parts_two, late.total, parts_late, qkv_state, vec_state)
     else:
         ones, twos = sum_one.full(), sum_two.full()
@@ -891,7 +920,7 @@
         new_down = update(down_state, grads[4], matrix_rate, weight_decay)
     return (
         result.reshape(tokens.shape),
-        final.input_grad.reshape(tokens.shape),
+        input_grad.reshape(tokens.shape),
         *new_qkv,
         *new_out,
         *new_up,

time: 140 us -> 128 us (0.914)
  waiting for transfers between devices: 36.6 us -> 24.3 us
    ppermute x39, waiting for transfers between devices: 36.6 us -> 24.3 us  [exchange(): return lax.ppermute(values, AXES, pairs)]
    pallas_call x14, Pallas kernels: 56 us -> 54.6 us  [call(): pl.pallas_call(kernel, out_shape=[(pltpu.VMEM if entry in IN_VMEM and len...]
  transfers between devices with their start and end apart: 39 -> 39, of which waited for: 18 -> 16; matrix products, arithmetic and copies ran while one was open for 0% -> 1% of each run, Pallas kernels for 43% -> 45%
where the time goes in v1:
time: 128 us
  Pallas kernels  60.7 us (47%)
  starting transfers between devices  40.6 us (32%)
  waiting for transfers between devices  24.3 us (19%)
  between operations  1.36 us (1%)
    pallas_call x14, Pallas kernels, call(): pl.pallas_call(kernel, out_shape=[(pltpu.VMEM if entry in IN_VMEM and len...  54.6 us
    ppermute x39, starting transfers between devices, exchange(): return lax.ppermute(values, AXES, pairs)  40.6 us
    ppermute x39, waiting for transfers between devices, exchange(): return lax.ppermute(values, AXES, pairs)  24.3 us
    pallas_call x1, Pallas kernels, hidden_update(): pl.pallas_call(hidden_update_kernel, out_shape=outs, in_specs=[whole()] *...  2.7 us
  transfers between devices with their start and end apart: 39, of which 16 were waited for; matrix products, arithmetic and copies ran while one was open for 1% of the time, Pallas kernels for 45%

profile of v1, /device:TPU:0, one launch (start us, length us, event | category | flops | bytes accessed | tf_op | source)
XLA Modules:
  0.0 127.8 jit_solution(1315997339001237535)
XLA Ops:
  2.2 5.1 %collective-permute-start.2 = (bf16[16,1664]{1,0:T(8,128)(2,1)S(1)}, bf16[16,1664]{1,0:T(8,128)(2,1)S(1)}, u32[]{:S(2)}, u32[]{:S(2)}) collective-permute-start(bf16[16,1664]{1,0:T(8,128)(2,1)S(1)} %get-tuple-element.133), channel_id=1, source_target_pairs={{0,24},{1,25},{2,26},{3,27},{4,28},{5,29},{6,30},{7,31},{8,16},{9,... | collective-permute-start | bytes 159752 | tf_op jit(solution)/shard_map/ppermute | solution.py:617
  9.6 2.7 %collective-permute-done.1 = bf16[16,1664]{1,0:T(8,128)(2,1)S(1)} collective-permute-done((bf16[16,1664]{1,0:T(8,128)(2,1)S(1)}, bf16[16,1664]{1,0:T(8,128)(2,1)S(1)}, u32[]{:S(2)}, u32[]{:S(2)}) %collective-permute-start.1) | collective-permute-done | bytes 53280 | tf_op jit(solution)/shard_map/ppermute | solution.py:617
  14.0 2.4 %collective-permute-start.14 = (bf16[16,2560]{1,0:T(8,128)(2,1)S(1)}, bf16[16,2560]{1,0:T(8,128)(2,1)S(1)}, u32[]{:S(2)}, u32[]{:S(2)}) collective-permute-start(bf16[16,2560]{1,0:T(8,128)(2,1)S(1)} %slice.31), channel_id=1, source_target_pairs={{0,24},{1,25},{2,26},{3,27},{4,28},{5,29},{6,30},{7,31},{8,16},{9,... | collective-permute-start | bytes 245768 | tf_op jit(solution)/shard_map/ppermute | solution.py:617
  16.5 2.0 %collective-permute-start.12 = (bf16[16,2560]{1,0:T(8,128)(2,1)S(1)}, bf16[16,2560]{1,0:T(8,128)(2,1)S(1)}, u32[]{:S(2)}, u32[]{:S(2)}) collective-permute-start(bf16[16,2560]{1,0:T(8,128)(2,1)S(1)} %slice.31), channel_id=1, source_target_pairs={{0,8},{1,9},{2,10},{3,11},{4,12},{5,13},{6,14},{7,15},{8,0},{9,1},... | collective-permute-start | bytes 245768 | tf_op jit(solution)/shard_map/ppermute | solution.py:617
  21.3 2.9 %collective-permute-done.13 = bf16[16,2560]{1,0:T(8,128)(2,1)S(1)} collective-permute-done((bf16[16,2560]{1,0:T(8,128)(2,1)S(1)}, bf16[16,2560]{1,0:T(8,128)(2,1)S(1)}, u32[]{:S(2)}, u32[]{:S(2)}) %collective-permute-start.13) | collective-permute-done | bytes 81952 | tf_op jit(solution)/shard_map/ppermute | solution.py:617
  25.8 2.7 %collective-permute-start.10 = (bf16[16,2048]{1,0:T(8,128)(2,1)S(1)}, bf16[16,2048]{1,0:T(8,128)(2,1)S(1)}, u32[]{:S(2)}, u32[]{:S(2)}) collective-permute-start(bf16[16,2048]{1,0:T(8,128)(2,1)S(1)} %slice.30), channel_id=1, source_target_pairs={{0,24},{1,25},{2,26},{3,27},{4,28},{5,29},{6,30},{7,31},{8,16},{9,... | collective-permute-start | bytes 196616 | tf_op jit(solution)/shard_map/ppermute | solution.py:617
  33.4 5.0 %attention.2 = (bf16[512,512]{1,0:T(8,128)(2,1)S(1)}, bf16[512,1536]{1,0:T(8,128)(2,1)S(1)}, bf16[512,512]{1,0:T(8,128)(2,1)S(1)}, f32[2,4,512]{2,1,0:T(4,128)S(...) custom-call(s32[1]{0:T(128)} %bitcast.refs_0_, s32[4]{0:T(128)S(1)} %copy-done.2, s32[4]{0:T(128)S(1)} %copy-done.1, ...), custom_call_target="tpu_custom_call" | custom-call | flops 8280000000 | tf_op jit(solution)/shard_map/attention/pallas_call | solution.py:80
  39.5 5.0 %attention.3 = (bf16[1024,512]{1,0:T(8,128)(2,1)S(1)}, bf16[1024,1536]{1,0:T(8,128)(2,1)S(1)}, bf16[1024,512]{1,0:T(8,128)(2,1)S(1)}, f32[4,4,512]{2,1,0:T(4,128)S(1)}) custom-call(s32[1]{0:T(128)} %bitcast.refs_0_, s32[4]{0:T(128)S(1)} %copy-done.2, s32[4]{0:T(128)S(1)} %copy-done.1, s32[4,1,256]{2,1,0:T(1,128)S(1)} %reshape.50.refs_3_.refs_2_, ...), custom_call_target="tpu_custom_call" | custom-call | flops 690000000 | tf_op jit(solution)/shard_map/attention/pallas_call | solution.py:80
  46.7 6.9 %hidden0.1 = (f32[1024,512]{1,0:T(8,128)S(1)}, bf16[1024,512]{1,0:T(8,128)(2,1)S(1)}, f32[1024,512]{1,0:T(8,128)S(1)}, bf16[512,512]{1,0:T(8,128)(2,1)S(1)}, bf1...) custom-call(s32[1]{0:T(128)} %bitcast.refs_0_, ...), custom_call_target="tpu_custom_call" | custom-call | flops 11729999872 | tf_op jit(solution)/shard_map/hidden0/pallas_call | solution.py:80
  54.6 4.3 %hidden1.1 = (f32[1024,512]{1,0:T(8,128)S(1)}, bf16[1024,512]{1,0:T(8,128)(2,1)S(1)}, bf16[512,512]{1,0:T(8,128)(2,1)S(1)}, f32[256,2048]{1,0:T(8,128)S(1)}, bf16[256,2048]{1,0:T(8,128)(2,1)S(1)}) custom-call(s32[1]{0:T(128)} %bitcast.refs_0_, bf16[1024,512]{1,0:T(8,128)(2,1)S(1)} %bitcast.10, ...), custom_call_target="tpu_custom_call", output_to_operand_aliasing={{0}: (3, {})} | custom-call | flops 8970000384 | tf_op jit(solution)/shard_map/hidden1/pallas_call | solution.py:80
  59.5 4.1 %hidden2.1 = (f32[1024,512]{1,0:T(8,128)S(1)}, bf16[1024,512]{1,0:T(8,128)(2,1)S(1)}, bf16[512,512]{1,0:T(8,128)(2,1)S(1)}, f32[512,512]{1,0:T(8,128)S(1)}, f32[512,512]{1,0:T(8,128)S(1)}) custom-call(s32[1]{0:T(128)} %bitcast.refs_0_, bf16[1024,512]{1,0:T(8,128)(2,1)S(1)} %bitcast.11, ...), custom_call_target="tpu_custom_call", output_to_operand_aliasing={{0}: (3, {})} | custom-call | flops 8970000384 | tf_op jit(solution)/shard_map/hidden2/pallas_call | solution.py:80
  65.3 4.1 %hidden3.1 = (f32[1024,512]{1,0:T(8,128)S(1)}, bf16[1024,512]{1,0:T(8,128)(2,1)S(1)}, bf16[512,512]{1,0:T(8,128)(2,1)S(1)}, f32[512,512]{1,0:T(8,128)S(1)}, f32[512,512]{1,0:T(8,128)S(1)}) custom-call(s32[1]{0:T(128)} %bitcast.refs_0_, bf16[1024,512]{1,0:T(8,128)(2,1)S(1)} %bitcast.12, ...), custom_call_target="tpu_custom_call", output_to_operand_aliasing={{0}: (3, {})} | custom-call | flops 8970000384 | tf_op jit(solution)/shard_map/hidden3/pallas_call | solution.py:80
  69.4 3.3 %middle_back.1 = (f32[1024,512]{1,0:T(8,128)S(1)}, bf16[1024,512]{1,0:T(8,128)(2,1)S(1)}, f32[8,512]{1,0:T(8,128)S(1)}, f32[256,2560]{1,0:T(8,128)S(1)}, bf16[256,2560]{1,0:T(8,128)(2,1)S(1)}) custom-call(s32[1]{0:T(128)} %bitcast.refs_0_, bf16[1024,512]{1,0:T(8,128)(2,1)S(1)} %bitcast.13, f32[8,512]{1,0:T(8,128)S(1)} %get-tuple-element.142.refs_6_.refs_5_.refs_2_.refs_4_, ...), custom_call_target="tpu_custom_call" | custom-call | flops 5520000000 | tf_op jit(solution)/shard_map/middle_back/pallas_call | solution.py:80
  74.3 3.8 %attention_back.4 = (bf16[1024,384]{1,0:T(8,128)(2,1)S(1)}, f32[512,384]{1,0:T(8,128)S(1)}) custom-call(s32[1]{0:T(128)} %bitcast.refs_0_, s32[4]{0:T(128)S(1)} %copy-done.1, bf16[1024,512]{1,0:T(8,128)(2,1)S(1)} %get-tuple-element.152.refs_2_.refs_6_, bf16[1024,1536]{1,0:T(8,128)(2,1)S(1)} %get-tuple-element.153.refs_3_, ...), custom_call_target="tpu_custom_call" | custom-call | flops 6347999744 | tf_op jit(solution)/shard_map/attention_back/pallas_call | solution.py:80
  81.4 3.6 %attention_back.6 = (bf16[1024,384]{1,0:T(8,128)(2,1)S(1)}, f32[256,768]{1,0:T(8,128)S(1)}, bf16[256,768]{1,0:T(8,128)(2,1)S(1)}) custom-call(s32[1]{0:T(128)} %bitcast.refs_0_, s32[4]{0:T(128)S(1)} %copy-done.1, bf16[1024,512]{1,0:T(8,128)(2,1)S(1)} %get-tuple-element.152.refs_2_.refs_6_, bf16[1024,1536]{1,0:T(8,128)(2,1)S(1)} %get-tuple-element.153.refs_3_, ...), custom_call_target="tpu_custom_call" | custom-call | flops 6347999744 | tf_op jit(solution)/shard_map/attention_back/pallas_call | solution.py:80
  85.1 3.6 %attention_back.5 = (bf16[1024,384]{1,0:T(8,128)(2,1)S(1)}, f32[512,384]{1,0:T(8,128)S(1)}) custom-call(s32[1]{0:T(128)} %bitcast.refs_0_, s32[4]{0:T(128)S(1)} %copy-done.1, bf16[1024,512]{1,0:T(8,128)(2,1)S(1)} %get-tuple-element.152.refs_2_.refs_6_, bf16[1024,1536]{1,0:T(8,128)(2,1)S(1)} %get-tuple-element.153.refs_3_, ...), custom_call_target="tpu_custom_call" | custom-call | flops 6347999744 | tf_op jit(solution)/shard_map/attention_back/pallas_call | solution.py:80
  90.9 2.8 %attention_back.7.refs_12_ = bf16[1024,384]{1,0:T(8,128)(2,1)S(1)} custom-call(s32[1]{0:T(128)} %bitcast.refs_0_, s32[4]{0:T(128)S(1)} %copy-done.1, bf16[1024,512]{1,0:T(8,128)(2,1)S(1)} %get-tuple-element.152.refs_2_.refs_6_, bf16[1024,1536]{1,0:T(8,128)(2,1)S(1)} %get-tuple-element.153.refs_3_, f32[4,4,512]{2,1,0:T(4,128)S(1)} %get-tuple-element.146.refs_4_, ...), custom_call_target="tpu_custom_call" | custom-call | flops 6347999744 | tf_op jit(solution)/shard_map/attention_back/pallas_call | solution.py:80
  95.6 4.5 %input_back.1 = (f32[1024,512]{1,0:T(8,128)S(1)}, f32[256,896]{1,0:T(8,128)S(1)}, bf16[256,896]{1,0:T(8,128)(2,1)S(1)}) custom-call(s32[1]{0:T(128)} %bitcast.refs_0_, s32[4]{0:T(128)S(1)} %copy-done.2, s32[4,1,256]{2,1,0:T(1,128)S(1)} %reshape.50.refs_3_.refs_2_, bf16[1024,512]{1,0:T(8,128)(2,1)S(1)} %bitcast.8, ...), custom_call_target="tpu_custom_call" | custom-call | flops 8970000384 | tf_op jit(solution)/shard_map/input_back/pallas_call | solution.py:80
  103.0 2.7 %collective-permute-start.33 = (bf16[16,5376]{1,0:T(8,128)(2,1)S(1)}, bf16[16,5376]{1,0:T(8,128)(2,1)S(1)}, u32[]{:S(2)}, u32[]{:S(2)}) collective-permute-start(bf16[16,5376]{1,0:T(8,128)(2,1)S(1)} %get-tuple-element.249), channel_id=1, source_target_pairs={{0,24},{1,25},{2,26},{3,27},{4,28},{5,29},{6,30},{7,31},{8,16},{9,... | collective-permute-start | bytes 516104 | tf_op jit(solution)/shard_map/ppermute | solution.py:617
  108.4 2.3 %branch_output.3 = (bf16[1024,512]{1,0:T(8,128)(2,1)}, f32[1024,512]{1,0:T(8,128)}) custom-call(f32[1024,512]{1,0:T(8,128)S(1)} %get-tuple-element.221.refs_4_.refs_0_, bf16[1024,512]{1,0:T(8,128)(2,1)S(1)} %get-tuple-element.211.refs_1_, bf16[512,512]{1,0:T(8,128)(2,1)S(1)} %get-tuple-element.212.refs_2_, bf16[1024,512]{1,0:T(8,128)(2,1)S(1)} %get-tuple-element.213.refs_3_, ...), custom_call_target="tpu_custom_call" | custom-call | flops 34500001792 | tf_op jit(solution)/shard_map/branch_output/pallas_call | solution.py:80
  110.7 3.0 %collective-permute-done.34.taken_ref = bf16[128,896]{1,0:T(8,128)(2,1)S(1)} collective-permute-done((bf16[128,896]{1,0:T(8,128)(2,1)S(1)}, bf16[128,896]{1,0:T(8,128)(2,1)S(1)}, u32[]{:S(2)}, u32[]{:S(2)}) %collective-permute-start.34) | collective-permute-done | bytes 229408 | tf_op jit(solution)/shard_map/ppermute | solution.py:617
  114.9 4.4 %collective-permute-done.32.refs_2_ = bf16[16,5376]{1,0:T(8,128)(2,1)S(1)} collective-permute-done((bf16[16,5376]{1,0:T(8,128)(2,1)S(1)}, bf16[16,5376]{1,0:T(8,128)(2,1)S(1)}, u32[]{:S(2)}, u32[]{:S(2)}) %collective-permute-start.32) | collective-permute-done | bytes 172064 | tf_op jit(solution)/shard_map/ppermute | solution.py:617
  119.4 2.8 %collective-permute-start.38 = (bf16[16,896]{1,0:T(8,128)(2,1)S(1)}, bf16[16,896]{1,0:T(8,128)(2,1)S(1)}, u32[]{:S(2)}, u32[]{:S(2)}) collective-permute-start(bf16[16,896]{1,0:T(8,128)(2,1)S(1)} %get-tuple-element.252), channel_id=1, source_target_pairs={{0,24},{1,25},{2,26},{3,27},{4,28},{5,29},{6,30},{7,31},{8,16},{9,... | collective-permute-start | bytes 86024 | tf_op jit(solution)/shard_map/ppermute | solution.py:617
  124.0 2.7 %hidden_update.1 = (f32[16,2048]{1,0:T(8,128)}, f32[16,2048]{1,0:T(8,128)}, f32[16,2048]{1,0:T(8,128)}, f32[64,512]{1,0:T(8,128)}, f32[64,512]{1,0:T(8,128)}, /*...) custom-call(f32[64,5376]{1,0:T(8,128)S(1)} %pad_maximum_fusion.refs_0_, ...), custom_call_target="tpu_custom_call" | custom-call | flops 4140000000 | tf_op jit(solution)/shard_map/hidden_update/pallas_call | solution.py:563
  (151 shorter events, 39.6 us)
Async XLA Ops:
  2.2 7.4 %collective-permute-start.2 = (bf16[16,1664]{1,0:T(8,128)(2,1)S(1)}, bf16[16,1664]{1,0:T(8,128)(2,1)S(1)}, u32[]{:S(2)}, u32[]{:S(2)}) collective-permute-start(bf16[16,1664]{1,0:T(8,128)(2,1)S(1)} %get-tuple-element.133), channel_id=1, source_target_pairs={{0,24},{1,25},{2,26},{3,27},{4,28},{5,29},{6,30},{7,31},{8,16},{9,... | collective-permute-start | bytes 159752 | tf_op jit(solution)/shard_map/ppermute | solution.py:617
  14.0 7.2 %collective-permute-start.14 = (bf16[16,2560]{1,0:T(8,128)(2,1)S(1)}, bf16[16,2560]{1,0:T(8,128)(2,1)S(1)}, u32[]{:S(2)}, u32[]{:S(2)}) collective-permute-start(bf16[16,2560]{1,0:T(8,128)(2,1)S(1)} %slice.31), channel_id=1, source_target_pairs={{0,24},{1,25},{2,26},{3,27},{4,28},{5,29},{6,30},{7,31},{8,16},{9,... | collective-permute-start | bytes 245768 | tf_op jit(solution)/shard_map/ppermute | solution.py:617
  16.5 7.7 %collective-permute-start.13 = (bf16[16,2560]{1,0:T(8,128)(2,1)S(1)}, bf16[16,2560]{1,0:T(8,128)(2,1)S(1)}, u32[]{:S(2)}, u32[]{:S(2)}) collective-permute-start(bf16[16,2560]{1,0:T(8,128)(2,1)S(1)} %slice.31), channel_id=1, source_target_pairs={{0,16},{1,17},{2,18},{3,19},{4,20},{5,21},{6,22},{7,23},{8,24},{9,... | collective-permute-start | bytes 245768 | tf_op jit(solution)/shard_map/ppermute | solution.py:617
  16.5 7.7 %collective-permute-start.12 = (bf16[16,2560]{1,0:T(8,128)(2,1)S(1)}, bf16[16,2560]{1,0:T(8,128)(2,1)S(1)}, u32[]{:S(2)}, u32[]{:S(2)}) collective-permute-start(bf16[16,2560]{1,0:T(8,128)(2,1)S(1)} %slice.31), channel_id=1, source_target_pairs={{0,8},{1,9},{2,10},{3,11},{4,12},{5,13},{6,14},{7,15},{8,0},{9,1},... | collective-permute-start | bytes 245768 | tf_op jit(solution)/shard_map/ppermute | solution.py:617
  18.5 7.3 %collective-permute-start.4 = (bf16[64,1664]{1,0:T(8,128)(2,1)S(1)}, bf16[64,1664]{1,0:T(8,128)(2,1)S(1)}, u32[]{:S(2)}, u32[]{:S(2)}) collective-permute-start(bf16[64,1664]{1,0:T(8,128)(2,1)S(1)} %collective-permute-done.3), channel_id=1, source_target_pairs={{0,1},{1,0},{2,3},{3,2},{4,5},{5,4},{6,7},{7,6},{8,9},{9,8},{10,11... | collective-permute-start | bytes 638984 | tf_op jit(solution)/shard_map/ppermute | solution.py:617
  18.6 11.7 %collective-permute-start.6 = (bf16[128,1664]{1,0:T(8,128)(2,1)S(1)}, bf16[128,1664]{1,0:T(8,128)(2,1)S(1)}, u32[]{:S(2)}, u32[]{:S(2)}) collective-permute-start(bf16[128,1664]{1,0:T(8,128)(2,1)S(1)} %constant_dynamic-update-slice_fusion.refs_5_), channel_id=1, source_target_pairs={{0,2},{1,5},{2,0},{3,7},{4,6},{5,1},{6,4},{7,3},{8,10},{9,13},{10,... | collective-permute-start | bytes 1277960 | tf_op jit(solution)/shard_map/ppermute | solution.py:617
  24.2 7.1 %collective-permute-start.15 = (bf16[64,2560]{1,0:T(8,128)(2,1)S(1)}, bf16[64,2560]{1,0:T(8,128)(2,1)S(1)}, u32[]{:S(2)}, u32[]{:S(2)}) collective-permute-start(bf16[64,2560]{1,0:T(8,128)(2,1)S(1)} %pad_maximum_fusion.3), channel_id=1, source_target_pairs={{0,4},{1,3},{2,6},{3,1},{4,0},{5,7},{6,2},{7,5},{8,12},{9,11},{10,... | collective-permute-start | bytes 983048 | tf_op jit(solution)/shard_map/ppermute | solution.py:617
  25.8 12.7 %collective-permute-start.10 = (bf16[16,2048]{1,0:T(8,128)(2,1)S(1)}, bf16[16,2048]{1,0:T(8,128)(2,1)S(1)}, u32[]{:S(2)}, u32[]{:S(2)}) collective-permute-start(bf16[16,2048]{1,0:T(8,128)(2,1)S(1)} %slice.30), channel_id=1, source_target_pairs={{0,24},{1,25},{2,26},{3,27},{4,28},{5,29},{6,30},{7,31},{8,16},{9,... | collective-permute-start | bytes 196616 | tf_op jit(solution)/shard_map/ppermute | solution.py:617
  28.5 10.0 %collective-permute-start.9 = (bf16[16,2048]{1,0:T(8,128)(2,1)S(1)}, bf16[16,2048]{1,0:T(8,128)(2,1)S(1)}, u32[]{:S(2)}, u32[]{:S(2)}) collective-permute-start(bf16[16,2048]{1,0:T(8,128)(2,1)S(1)} %slice.30), channel_id=1, source_target_pairs={{0,16},{1,17},{2,18},{3,19},{4,20},{5,21},{6,22},{7,23},{8,24},{9,... | collective-permute-start | bytes 196616 | tf_op jit(solution)/shard_map/ppermute | solution.py:617
  28.5 10.0 %collective-permute-start.5 = (bf16[16,2048]{1,0:T(8,128)(2,1)S(1)}, bf16[16,2048]{1,0:T(8,128)(2,1)S(1)}, u32[]{:S(2)}, u32[]{:S(2)}) collective-permute-start(bf16[16,2048]{1,0:T(8,128)(2,1)S(1)} %slice.30), channel_id=1, source_target_pairs={{0,8},{1,9},{2,10},{3,11},{4,12},{5,13},{6,14},{7,15},{8,0},{9,1},... | collective-permute-start | bytes 196616 | tf_op jit(solution)/shard_map/ppermute | solution.py:617
  31.4 13.2 %collective-permute-start.17 = (bf16[128,2560]{1,0:T(8,128)(2,1)S(1)}, bf16[128,2560]{1,0:T(8,128)(2,1)S(1)}, u32[]{:S(2)}, u32[]{:S(2)}) collective-permute-start(bf16[128,2560]{1,0:T(8,128)(2,1)S(1)} %constant_dynamic-update-slice_fusion.5.refs_7_.refs_4_), channel_id=1, source_target_pairs={{0,1},{1,0},{2,3},{3,2},{4,5},{5,4},{6,7},{7,6},{8,9},{9,8},{10,11... | collective-permute-start | bytes 1966088 | tf_op jit(solution)/shard_map/ppermute | solution.py:617
  32.2 12.3 %collective-permute-start.16 = (bf16[128,2560]{1,0:T(8,128)(2,1)S(1)}, bf16[128,2560]{1,0:T(8,128)(2,1)S(1)}, u32[]{:S(2)}, u32[]{:S(2)}) collective-permute-start(bf16[128,2560]{1,0:T(8,128)(2,1)S(1)} %constant_dynamic-update-slice_fusion.5.refs_7_.refs_4_), channel_id=1, source_target_pairs={{0,2},{1,5},{2,0},{3,7},{4,6},{5,1},{6,4},{7,3},{8,10},{9,13},{10,... | collective-permute-start | bytes 1966088 | tf_op jit(solution)/shard_map/ppermute | solution.py:617
  45.0 8.6 %collective-permute-start.21 = (bf16[128,2048]{1,0:T(8,128)(2,1)S(1)}, bf16[128,2048]{1,0:T(8,128)(2,1)S(1)}, u32[]{:S(2)}, u32[]{:S(2)}) collective-permute-start(bf16[128,2048]{1,0:T(8,128)(2,1)S(1)} %constant_dynamic-update-slice_fusion.10.refs_4_), channel_id=1, source_target_pairs={{0,1},{1,0},{2,3},{3,2},{4,5},{5,4},{6,7},{7,6},{8,9},{9,8},{10,11... | collective-permute-start | bytes 1572872 | tf_op jit(solution)/shard_map/ppermute | solution.py:617
  45.5 9.2 %collective-permute-start.20 = (bf16[128,2048]{1,0:T(8,128)(2,1)S(1)}, bf16[128,2048]{1,0:T(8,128)(2,1)S(1)}, u32[]{:S(2)}, u32[]{:S(2)}) collective-permute-start(bf16[128,2048]{1,0:T(8,128)(2,1)S(1)} %constant_dynamic-update-slice_fusion.10.refs_4_), channel_id=1, source_target_pairs={{0,2},{1,5},{2,0},{3,7},{4,6},{5,1},{6,4},{7,3},{8,10},{9,13},{10,... | collective-permute-start | bytes 1572872 | tf_op jit(solution)/shard_map/ppermute | solution.py:617
  63.9 9.2 %collective-permute-start.24 = (bf16[128,2048]{1,0:T(8,128)(2,1)S(1)}, bf16[128,2048]{1,0:T(8,128)(2,1)S(1)}, u32[]{:S(2)}, u32[]{:S(2)}) collective-permute-start(bf16[128,2048]{1,0:T(8,128)(2,1)S(1)} %get-tuple-element.167), channel_id=1, source_target_pairs={{0,2},{1,5},{2,0},{3,7},{4,6},{5,1},{6,4},{7,3},{8,10},{9,13},{10,... | collective-permute-start | bytes 1572872 | tf_op jit(solution)/shard_map/ppermute | solution.py:617
  72.7 7.1 %collective-permute-start.23 = (bf16[256,2560]{1,0:T(8,128)(2,1)S(1)}, bf16[256,2560]{1,0:T(8,128)(2,1)S(1)}, u32[]{:S(2)}, u32[]{:S(2)}) collective-permute-start(bf16[256,2560]{1,0:T(8,128)(2,1)S(1)} %get-tuple-element.178), channel_id=1, source_target_pairs={{0,1},{1,0},{2,3},{3,2},{4,5},{5,4},{6,7},{7,6},{8,9},{9,8},{10,11... | collective-permute-start | bytes 3932168 | tf_op jit(solution)/shard_map/ppermute | solution.py:617
  73.3 6.4 %collective-permute-start.26 = (bf16[64,2048]{1,0:T(8,128)(2,1)S(1)}, bf16[64,2048]{1,0:T(8,128)(2,1)S(1)}, u32[]{:S(2)}, u32[]{:S(2)}) collective-permute-start(bf16[64,2048]{1,0:T(8,128)(2,1)S(1)} %get-tuple-element.186), channel_id=1, source_target_pairs={{0,4},{1,3},{2,6},{3,1},{4,0},{5,7},{6,2},{7,5},{8,12},{9,11},{10,... | collective-permute-start | bytes 786440 | tf_op jit(solution)/shard_map/ppermute | solution.py:617
  80.1 10.7 %collective-permute-start.25 = (bf16[128,2560]{1,0:T(8,128)(2,1)S(1)}, bf16[128,2560]{1,0:T(8,128)(2,1)S(1)}, u32[]{:S(2)}, u32[]{:S(2)}) collective-permute-start(bf16[128,2560]{1,0:T(8,128)(2,1)S(1)} %get-tuple-element.185), channel_id=1, source_target_pairs={{0,2},{1,5},{2,0},{3,7},{4,6},{5,1},{6,4},{7,3},{8,10},{9,13},{10,... | collective-permute-start | bytes 1966088 | tf_op jit(solution)/shard_map/ppermute | solution.py:617
  94.6 8.2 %collective-permute-start.30 = (bf16[64,3328]{1,0:T(8,128)(2,1)S(1)}, bf16[64,3328]{1,0:T(8,128)(2,1)S(1)}, u32[]{:S(2)}, u32[]{:S(2)}) collective-permute-start(bf16[64,3328]{1,0:T(8,128)(2,1)S(1)} %pad_maximum_fusion.2), channel_id=1, source_target_pairs={{0,4},{1,3},{2,6},{3,1},{4,0},{5,7},{6,2},{7,5},{8,12},{9,11},{10,... | collective-permute-start | bytes 1277960 | tf_op jit(solution)/shard_map/ppermute | solution.py:617
  100.1 7.4 %collective-permute-start.29 = (bf16[256,896]{1,0:T(8,128)(2,1)S(1)}, bf16[256,896]{1,0:T(8,128)(2,1)S(1)}, u32[]{:S(2)}, u32[]{:S(2)}) collective-permute-start(bf16[256,896]{1,0:T(8,128)(2,1)S(1)} %get-tuple-element.208), channel_id=1, source_target_pairs={{0,1},{1,0},{2,3},{3,2},{4,5},{5,4},{6,7},{7,6},{8,9},{9,8},{10,11... | collective-permute-start | bytes 1376264 | tf_op jit(solution)/shard_map/ppermute | solution.py:617
  103.0 11.9 %collective-permute-start.33 = (bf16[16,5376]{1,0:T(8,128)(2,1)S(1)}, bf16[16,5376]{1,0:T(8,128)(2,1)S(1)}, u32[]{:S(2)}, u32[]{:S(2)}) collective-permute-start(bf16[16,5376]{1,0:T(8,128)(2,1)S(1)} %get-tuple-element.249), channel_id=1, source_target_pairs={{0,24},{1,25},{2,26},{3,27},{4,28},{5,29},{6,30},{7,31},{8,16},{9,... | collective-permute-start | bytes 516104 | tf_op jit(solution)/shard_map/ppermute | solution.py:617
  105.7 13.6 %collective-permute-start.32 = (bf16[16,5376]{1,0:T(8,128)(2,1)S(1)}, bf16[16,5376]{1,0:T(8,128)(2,1)S(1)}, u32[]{:S(2)}, u32[]{:S(2)}) collective-permute-start(bf16[16,5376]{1,0:T(8,128)(2,1)S(1)} %get-tuple-element.250), channel_id=1, source_target_pairs={{0,16},{1,17},{2,18},{3,19},{4,20},{5,21},{6,22},{7,23},{8,24},{9,... | collective-permute-start | bytes 516104 | tf_op jit(solution)/shard_map/ppermute | solution.py:617
  105.7 13.6 %collective-permute-start.31 = (bf16[16,5376]{1,0:T(8,128)(2,1)S(1)}, bf16[16,5376]{1,0:T(8,128)(2,1)S(1)}, u32[]{:S(2)}, u32[]{:S(2)}) collective-permute-start(bf16[16,5376]{1,0:T(8,128)(2,1)S(1)} %get-tuple-element.251), channel_id=1, source_target_pairs={{0,8},{1,9},{2,10},{3,11},{4,12},{5,13},{6,14},{7,15},{8,0},{9,1},... | collective-permute-start | bytes 516104 | tf_op jit(solution)/shard_map/ppermute | solution.py:617
  119.4 7.3 %collective-permute-start.38 = (bf16[16,896]{1,0:T(8,128)(2,1)S(1)}, bf16[16,896]{1,0:T(8,128)(2,1)S(1)}, u32[]{:S(2)}, u32[]{:S(2)}) collective-permute-start(bf16[16,896]{1,0:T(8,128)(2,1)S(1)} %get-tuple-element.252), channel_id=1, source_target_pairs={{0,24},{1,25},{2,26},{3,27},{4,28},{5,29},{6,30},{7,31},{8,16},{9,... | collective-permute-start | bytes 86024 | tf_op jit(solution)/shard_map/ppermute | solution.py:617
  (35 other events, 248.1 us)

commit v2 on v1

--- a/solution.py
+++ b/solution.py
@@ -20,8 +20,8 @@
 SCALE = 1.2
 FIRST_HALF = 4 * QUARTER + D + 6 * LANES
 REAR_COST = 0.5
+AHEAD = (0,)
 IN_VMEM = ("input_grad",)
-UNROLL = 2
 VMEM_BYTES = 16 * 1024 * 1024
 
 norm_epsilon = 1e-05
@@ -182,13 +182,18 @@
     return masked, jnp.where(masked, r.vec[4:5, :], wide(r.tokens[rows, :]))
 
 
-def each_span(seq, spans, body):
+def each_span(seq, spans, body, ahead=None):
     def step(index, carry):
-        span = spans[0] + index
-        body(span, pl.ds(pl.multiple_of(span * seq, seq), seq))
+        here = []
+        for n in range(2):
+            span = spans[0] + 2 * index + n
+            here.append((span, pl.ds(pl.multiple_of(span * seq, seq), seq)))
+        made = [ahead(span, rows) if ahead is not None else None for span, rows in here]
+        for (span, rows), value in zip(here, made):
+            body(span, rows, value)
         return carry
 
-    lax.fori_loop(0, len(spans), step, 0, unroll=UNROLL)
+    lax.fori_loop(0, len(spans) // 2, step, 0)
 
 
 def attention(scalar, order, tokens, first, spans, front=None):
@@ -206,27 +211,34 @@
                 getattr(r, name)[pl.ds(0, old.shape[0]), :] = old[...]
             r.logs[: spans[0]] = r.front_logs[...]
 
-        def one_span(span, rows):
+        def project(span, rows):
             started = load_input(r, span, rows)[1]
             normed = low(centre(started)[0] * r.vec[0:1, :] + r.vec[2:3, :])
             r.normed[rows, :] = normed
             r.p[rows, :] = low(dot(normed, r.weight[...]))
+
+        def one_span(span, rows, made):
+            def scored(pair):
+                queries = pair_split(r.p[rows, pl.ds(pair * LANES, LANES)], HEAD**-0.5)
+                return key_scores(r.p[rows, pl.ds(D + pair * LANES, LANES)], queries, r.length[span])
+
+            ahead = scored(0)
             for pair in range(PAIRS):
-                lanes = pl.ds(pair * LANES, LANES)
-                queries = pair_split(r.p[rows, lanes], HEAD**-0.5)
-                scores = key_scores(r.p[rows, pl.ds(D + pair * LANES, LANES)], queries, r.length[span])
+                scores = ahead
+                if pair + 1 < PAIRS:
+                    ahead = scored(pair + 1)
                 peak = jnp.max(scores, axis=0, keepdims=True)
                 exped = jnp.exp(scores - peak)
                 total = jnp.sum(exped, axis=0, keepdims=True)
-                probability = low(exped / total)
+                probability = low(exped * (1.0 / total))
                 r.logs[span, pair : pair + 1, :] = peak + jnp.log(total)
                 values = jnp.transpose(r.p[rows, pl.ds(2 * D + pair * LANES, LANES)])
                 attended = jnp.concatenate(
                     [dot(values[:HEAD], probability[:, :seq]), dot(values[HEAD:], probability[:, seq:])], axis=0
                 )
-                r.attended[rows, lanes] = jnp.transpose(low(attended))
-
-        each_span(seq, spans, one_span)
+                r.attended[rows, pl.ds(pair * LANES, LANES)] = jnp.transpose(low(attended))
+
+        each_span(seq, spans, one_span, project)
 
     ins = [(name, array, scalars()) for name, array in scalar.items()] + [("order", order), ("tokens", tokens)]
     count = spans[-1] + 1
@@ -248,16 +260,33 @@
     return call(body, "attention", 6 if fresh else REAR_COST, ins, outs, scratch)
 
 
-def hidden_quarter(normed, upstream, up, down):
-    hidden = dot(normed, up)
-    grad_act = dot_rows(upstream, down)
+def hidden_units(hidden, grad_act):
     squared = hidden * hidden
     tilt = jnp.tanh(hidden * (gelu_scale + (gelu_scale * gelu_cubic) * squared))
     gate = 0.5 + 0.5 * tilt
     active = hidden * gate
     slope = gate + active * (1.0 - tilt) * (gelu_scale + (3.0 * gelu_scale * gelu_cubic) * squared)
-    grad_hidden = low(grad_act * slope)
-    return low(active), grad_hidden, dot_rows(grad_hidden, up)
+    return low(active), low(grad_act * slope)
+
+
+def products_ahead(r, seq, total):
+    def products(columns, rows):
+        hidden = dot(r.middle_normed[rows, :], r.up[:, columns])
+        return hidden, dot_rows(r.cot[rows, :], r.down_full[columns, :])
+
+    spans = [pl.ds(span * seq, seq) for span in range(total // seq)]
+    todo = [(pl.ds(first, 2 * LANES), rows) for first in range(0, QUARTER, 2 * LANES) for rows in spans]
+    ahead = products(*todo[0])
+    for n, (columns, rows) in enumerate(todo):
+        here = ahead
+        if n + 1 < len(todo):
+            ahead = products(*todo[n + 1])
+        active, grad_hidden = hidden_units(*here)
+        r.active[rows, columns] = active
+        r.grad_hidden[rows, columns] = grad_hidden
+        if (n + 1) % len(spans) == 0:
+            r.grad_up[:, columns] = dot_columns(r.middle_normed[...], r.grad_hidden[:, columns])
+            r.grad_down[columns, :] = dot_columns(r.active[:, columns], r.cot[...])
 
 
 def quarter_call(quarter, scalar, cotangent, stacks, ins, outs, seq, before, after, micros, reused=(), mate=None):
@@ -271,16 +300,28 @@
             targets.append((r.out_full, 4 * QUARTER))
         assemble(r.me[0], stacks, targets)
 
-        def one_span(span, rows):
-            normed = before(r, span, rows)
-            active, grad_hidden, back = hidden_quarter(normed, r.cot[rows, :], r.up[...], r.down_full[...])
-            r.active[rows, :] = active
-            r.grad_hidden[rows, :] = grad_hidden
-            after(r, rows, back)
-
-        each_span(seq, range(total // seq), one_span)
-        r.grad_up[...] = dot_columns(r.middle_normed[...], r.grad_hidden[...])
-        r.grad_down[...] = dot_columns(r.active[...], r.cot[...])
+        if quarter not in AHEAD:
+            def products(span, rows):
+                return dot(before(r, span, rows), r.up[...]), dot_rows(r.cot[rows, :], r.down_full[...])
+
+            def one_span(span, rows, made):
+                active, grad_hidden = hidden_units(*made)
+                r.active[rows, :] = active
+                r.grad_hidden[rows, :] = grad_hidden
+                after(r, rows, dot_rows(grad_hidden, r.up[...]))
+
+            each_span(seq, range(total // seq), one_span, products)
+            r.grad_up[...] = dot_columns(r.middle_normed[...], r.grad_hidden[...])
+            r.grad_down[...] = dot_columns(r.active[...], r.cot[...])
+        else:
+
+            def enter(span, rows, made):
+                before(r, span, rows)
+
+            if quarter == 0:
+                each_span(seq, range(total // seq), enter)
+            products_ahead(r, seq, total)
+            after(r, slice(None), dot_rows(r.grad_hidden[...], r.up[...]))
         if mate is not None:
             arrange(r.me[0], (r.mate_up, r.mate_down, r.grad_up, r.grad_down), r.keep, r.send)
 
@@ -339,7 +380,7 @@
     def body(r):
         r.dvec[...] = jnp.zeros_like(r.dvec)
 
-        def one_span(span, rows):
+        def one_span(span, rows, made):
             back = r.back[rows, :]
             hat, scale = centre(r.middle[rows, :])
             dmiddle = wide(r.cot[rows, :]) + norm_back(back, r.vec[1:2, :], hat, scale)
@@ -381,7 +422,7 @@
             copies[1].start()
         target = r.result if front is None else r.rear
 
-        def one_span(span, rows):
+        def one_span(span, rows, made):
             result = r.middle[rows, :]
             for n in range(4):
                 result = result + dot(getattr(r, "active%d" % n)[rows, :], getattr(r, "down%d" % n)[...])
@@ -410,22 +451,24 @@
     last = pair == PAIRS - 1
 
     def body(r):
-        def one_span(span, rows):
+        def products(span, rows):
             queries = pair_split(r.p[rows, pl.ds(pair * LANES, LANES)], HEAD**-0.5)
             dattended = pair_split(r.dattended[rows, pl.ds(pair * LANES, LANES)])
-            keys = r.p[rows, pl.ds(D + pair * LANES, LANES)]
-            scores = key_scores(keys, queries, r.length[span])
+            scores = key_scores(r.p[rows, pl.ds(D + pair * LANES, LANES)], queries, r.length[span])
+            return queries, dattended, scores, dot_rows(r.p[rows, pl.ds(2 * D + pair * LANES, LANES)], dattended)
+
+        def one_span(span, rows, made):
+            queries, dattended, scores, dprobability = made
             probability = jnp.exp(scores - r.logs[span, pair : pair + 1, :])
-            dprobability = dot_rows(r.p[rows, pl.ds(2 * D + pair * LANES, LANES)], dattended)
             inner = jnp.sum(probability * dprobability, axis=0, keepdims=True)
             dscores = low(probability * (dprobability - inner))
             dvalues = low(dot(low(probability), dattended))
             dkeys = low(dot(dscores, queries))
-            keys = jnp.transpose(low(wide(keys) * HEAD**-0.5))
+            keys = jnp.transpose(low(wide(r.p[rows, pl.ds(D + pair * LANES, LANES)]) * HEAD**-0.5))
             dqueries = jnp.concatenate([dot(keys[:HEAD], dscores[:, :seq]), dot(keys[HEAD:], dscores[:, seq:])], axis=0)
             r.dp[rows, :] = jnp.concatenate([jnp.transpose(low(dqueries)), dkeys, dvalues], axis=1)
 
-        each_span(seq, range(total // seq), one_span)
+        each_span(seq, range(total // seq), one_span, products)
         if not last:
             r.grad[...] = dot_columns(r.normed[...], r.dp[...])
         if mate is not None:
@@ -454,9 +497,11 @@
         r.dvec[...] = jnp.zeros_like(r.dvec)
         r.dvec[:8, :] = r.dvec_in[...]
 
-        def one_span(span, rows):
+        def products(span, rows):
             dp = [part[rows, pl.ds(kind * LANES, LANES)] for kind in range(3) for part in parts]
-            back = dot_rows(jnp.concatenate(dp, axis=1), r.weight[...])
+            return dot_rows(jnp.concatenate(dp, axis=1), r.weight[...])
+
+        def one_span(span, rows, back):
             masked, started = load_input(r, span, rows)
             hat, scale = centre(started)
             dstarted = r.dmiddle[rows, :] + norm_back(back, r.vec[0:1, :], hat, scale)
@@ -465,7 +510,7 @@
             r.dvec[2:3, :] += jnp.sum(back, axis=0, keepdims=True)
             r.dvec[4:5, :] += jnp.sum(jnp.where(masked, dstarted, 0.0), axis=0, keepdims=True)
 
-        each_span(seq, range(total // seq), one_span)
+        each_span(seq, range(total // seq), one_span, products)
         r.columns[...] = jnp.transpose(r.dvec[...])
         r.grad[...] = dot_columns(r.normed[...], parts[-1][...])
         arrange(r.me[0], (r.mate, r.grad, r.columns), r.keep, r.send)

time: 128 us -> 128 us (level)
  Pallas kernels: 60.7 us -> 55.8 us
  waiting for transfers between devices: 24.3 us -> 28.8 us
    pallas_call x14, Pallas kernels: 54.6 us -> 49.7 us  [call(): pl.pallas_call(kernel, out_shape=[(pltpu.VMEM if entry in IN_VMEM and len...]
    ppermute x39, waiting for transfers between devices: 24.3 us -> 28.8 us  [exchange(): return lax.ppermute(values, AXES, pairs)]
  transfers between devices with their start and end apart: 39 -> 39, of which waited for: 16 -> 17; matrix products, arithmetic and copies ran while one was open for 1% -> 1% of each run, Pallas kernels for 45% -> 42%
where the time goes in v2:
time: 128 us
  Pallas kernels  55.8 us (44%)
  starting transfers between devices  40.8 us (32%)
  waiting for transfers between devices  28.8 us (22%)
  between operations  1.35 us (1%)
    pallas_call x14, Pallas kernels, call(): pl.pallas_call(kernel, out_shape=[(pltpu.VMEM if entry in IN_VMEM and len...  49.7 us
    ppermute x39, starting transfers between devices, exchange(): return lax.ppermute(values, AXES, pairs)  40.8 us
    ppermute x39, waiting for transfers between devices, exchange(): return lax.ppermute(values, AXES, pairs)  28.8 us
    pallas_call x1, Pallas kernels, hidden_update(): pl.pallas_call(hidden_update_kernel, out_shape=outs, in_specs=[whole()] *...  2.7 us
  transfers between devices with their start and end apart: 39, of which 17 were waited for; matrix products, arithmetic and copies ran while one was open for 1% of the time, Pallas kernels for 42%

profile of v2, /device:TPU:0, one launch (start us, length us, event | category | flops | bytes accessed | tf_op | source)
XLA Modules:
  0.0 127.5 jit_solution(16189129533506402537)
XLA Ops:
  2.2 5.1 %collective-permute-start.2 = (bf16[16,1664]{1,0:T(8,128)(2,1)S(1)}, bf16[16,1664]{1,0:T(8,128)(2,1)S(1)}, u32[]{:S(2)}, u32[]{:S(2)}) collective-permute-start(bf16[16,1664]{1,0:T(8,128)(2,1)S(1)} %get-tuple-element.133), channel_id=1, source_target_pairs={{0,24},{1,25},{2,26},{3,27},{4,28},{5,29},{6,30},{7,31},{8,16},{9,... | collective-permute-start | bytes 159752 | tf_op jit(solution)/shard_map/ppermute | solution.py:662
  9.6 2.7 %collective-permute-done.1 = bf16[16,1664]{1,0:T(8,128)(2,1)S(1)} collective-permute-done((bf16[16,1664]{1,0:T(8,128)(2,1)S(1)}, bf16[16,1664]{1,0:T(8,128)(2,1)S(1)}, u32[]{:S(2)}, u32[]{:S(2)}) %collective-permute-start.1) | collective-permute-done | bytes 53280 | tf_op jit(solution)/shard_map/ppermute | solution.py:662
  14.0 2.4 %collective-permute-start.14 = (bf16[16,2560]{1,0:T(8,128)(2,1)S(1)}, bf16[16,2560]{1,0:T(8,128)(2,1)S(1)}, u32[]{:S(2)}, u32[]{:S(2)}) collective-permute-start(bf16[16,2560]{1,0:T(8,128)(2,1)S(1)} %slice.31), channel_id=1, source_target_pairs={{0,24},{1,25},{2,26},{3,27},{4,28},{5,29},{6,30},{7,31},{8,16},{9,... | collective-permute-start | bytes 245768 | tf_op jit(solution)/shard_map/ppermute | solution.py:662
  21.3 2.9 %collective-permute-done.13 = bf16[16,2560]{1,0:T(8,128)(2,1)S(1)} collective-permute-done((bf16[16,2560]{1,0:T(8,128)(2,1)S(1)}, bf16[16,2560]{1,0:T(8,128)(2,1)S(1)}, u32[]{:S(2)}, u32[]{:S(2)}) %collective-permute-start.13) | collective-permute-done | bytes 81952 | tf_op jit(solution)/shard_map/ppermute | solution.py:662
  25.8 2.7 %collective-permute-start.10 = (bf16[16,2048]{1,0:T(8,128)(2,1)S(1)}, bf16[16,2048]{1,0:T(8,128)(2,1)S(1)}, u32[]{:S(2)}, u32[]{:S(2)}) collective-permute-start(bf16[16,2048]{1,0:T(8,128)(2,1)S(1)} %slice.30), channel_id=1, source_target_pairs={{0,24},{1,25},{2,26},{3,27},{4,28},{5,29},{6,30},{7,31},{8,16},{9,... | collective-permute-start | bytes 196616 | tf_op jit(solution)/shard_map/ppermute | solution.py:662
  33.4 4.2 %attention.2 = (bf16[512,512]{1,0:T(8,128)(2,1)S(1)}, bf16[512,1536]{1,0:T(8,128)(2,1)S(1)}, bf16[512,512]{1,0:T(8,128)(2,1)S(1)}, f32[2,4,512]{2,1,0:T(4,128)S(...) custom-call(s32[1]{0:T(128)} %bitcast.refs_0_, s32[4]{0:T(128)S(1)} %copy-done.2, s32[4]{0:T(128)S(1)} %copy-done.1, ...), custom_call_target="tpu_custom_call" | custom-call | flops 8280000000 | tf_op jit(solution)/shard_map/attention/pallas_call | solution.py:80
  38.6 4.1 %attention.3 = (bf16[1024,512]{1,0:T(8,128)(2,1)S(1)}, bf16[1024,1536]{1,0:T(8,128)(2,1)S(1)}, bf16[1024,512]{1,0:T(8,128)(2,1)S(1)}, f32[4,4,512]{2,1,0:T(4,128)S(1)}) custom-call(s32[1]{0:T(128)} %bitcast.refs_0_, s32[4]{0:T(128)S(1)} %copy-done.2, s32[4]{0:T(128)S(1)} %copy-done.1, s32[4,1,256]{2,1,0:T(1,128)S(1)} %reshape.50.refs_3_.refs_2_, ...), custom_call_target="tpu_custom_call" | custom-call | flops 690000000 | tf_op jit(solution)/shard_map/attention/pallas_call | solution.py:80
  42.7 2.6 %collective-permute-done.16.refs_8_.refs_5_ = bf16[128,2560]{1,0:T(8,128)(2,1)S(1)} collective-permute-done((bf16[128,2560]{1,0:T(8,128)(2,1)S(1)}, bf16[128,2560]{1,0:T(8,128)(2,1)S(1)}, u32[]{:S(2)}, u32[]{:S(2)}) %collective-permute-start.16) | collective-permute-done | bytes 655392 | tf_op jit(solution)/shard_map/ppermute | solution.py:662
  47.5 5.8 %hidden0.1 = (f32[1024,512]{1,0:T(8,128)S(1)}, bf16[1024,512]{1,0:T(8,128)(2,1)S(1)}, f32[1024,512]{1,0:T(8,128)S(1)}, bf16[512,512]{1,0:T(8,128)(2,1)S(1)}, bf1...) custom-call(s32[1]{0:T(128)} %bitcast.refs_0_, ...), custom_call_target="tpu_custom_call" | custom-call | flops 11729999872 | tf_op jit(solution)/shard_map/hidden0/pallas_call | solution.py:80
  55.2 4.1 %hidden1.1 = (f32[1024,512]{1,0:T(8,128)S(1)}, bf16[1024,512]{1,0:T(8,128)(2,1)S(1)}, bf16[512,512]{1,0:T(8,128)(2,1)S(1)}, f32[256,2048]{1,0:T(8,128)S(1)}, bf16[256,2048]{1,0:T(8,128)(2,1)S(1)}) custom-call(s32[1]{0:T(128)} %bitcast.refs_0_, bf16[1024,512]{1,0:T(8,128)(2,1)S(1)} %bitcast.10, ...), custom_call_target="tpu_custom_call", output_to_operand_aliasing={{0}: (3, {})} | custom-call | flops 8970000384 | tf_op jit(solution)/shard_map/hidden1/pallas_call | solution.py:80
  59.9 3.9 %hidden2.1 = (f32[1024,512]{1,0:T(8,128)S(1)}, bf16[1024,512]{1,0:T(8,128)(2,1)S(1)}, bf16[512,512]{1,0:T(8,128)(2,1)S(1)}, f32[512,512]{1,0:T(8,128)S(1)}, f32[512,512]{1,0:T(8,128)S(1)}) custom-call(s32[1]{0:T(128)} %bitcast.refs_0_, bf16[1024,512]{1,0:T(8,128)(2,1)S(1)} %bitcast.11, ...), custom_call_target="tpu_custom_call", output_to_operand_aliasing={{0}: (3, {})} | custom-call | flops 8970000384 | tf_op jit(solution)/shard_map/hidden2/pallas_call | solution.py:80
  65.4 3.9 %hidden3.1 = (f32[1024,512]{1,0:T(8,128)S(1)}, bf16[1024,512]{1,0:T(8,128)(2,1)S(1)}, bf16[512,512]{1,0:T(8,128)(2,1)S(1)}, f32[512,512]{1,0:T(8,128)S(1)}, f32[512,512]{1,0:T(8,128)S(1)}) custom-call(s32[1]{0:T(128)} %bitcast.refs_0_, bf16[1024,512]{1,0:T(8,128)(2,1)S(1)} %bitcast.12, ...), custom_call_target="tpu_custom_call", output_to_operand_aliasing={{0}: (3, {})} | custom-call | flops 8970000384 | tf_op jit(solution)/shard_map/hidden3/pallas_call | solution.py:80
  69.3 3.5 %middle_back.1 = (f32[1024,512]{1,0:T(8,128)S(1)}, bf16[1024,512]{1,0:T(8,128)(2,1)S(1)}, f32[8,512]{1,0:T(8,128)S(1)}, f32[256,2560]{1,0:T(8,128)S(1)}, bf16[256,2560]{1,0:T(8,128)(2,1)S(1)}) custom-call(s32[1]{0:T(128)} %bitcast.refs_0_, bf16[1024,512]{1,0:T(8,128)(2,1)S(1)} %bitcast.13, f32[8,512]{1,0:T(8,128)S(1)} %get-tuple-element.142.refs_6_.refs_5_.refs_2_.refs_4_, ...), custom_call_target="tpu_custom_call" | custom-call | flops 5520000000 | tf_op jit(solution)/shard_map/middle_back/pallas_call | solution.py:80
  74.4 3.2 %attention_back.4 = (bf16[1024,384]{1,0:T(8,128)(2,1)S(1)}, f32[512,384]{1,0:T(8,128)S(1)}) custom-call(s32[1]{0:T(128)} %bitcast.refs_0_, s32[4]{0:T(128)S(1)} %copy-done.1, bf16[1024,512]{1,0:T(8,128)(2,1)S(1)} %get-tuple-element.152.refs_2_.refs_6_, bf16[1024,1536]{1,0:T(8,128)(2,1)S(1)} %get-tuple-element.153.refs_3_, ...), custom_call_target="tpu_custom_call" | custom-call | flops 6347999744 | tf_op jit(solution)/shard_map/attention_back/pallas_call | solution.py:80
  77.6 2.3 %collective-permute-done.26 = bf16[64,2048]{1,0:T(8,128)(2,1)S(1)} collective-permute-done((bf16[64,2048]{1,0:T(8,128)(2,1)S(1)}, bf16[64,2048]{1,0:T(8,128)(2,1)S(1)}, u32[]{:S(2)}, u32[]{:S(2)}) %collective-permute-start.26) | collective-permute-done | bytes 262176 | tf_op jit(solution)/shard_map/ppermute | solution.py:662
  81.6 3.2 %attention_back.6 = (bf16[1024,384]{1,0:T(8,128)(2,1)S(1)}, f32[256,768]{1,0:T(8,128)S(1)}, bf16[256,768]{1,0:T(8,128)(2,1)S(1)}) custom-call(s32[1]{0:T(128)} %bitcast.refs_0_, s32[4]{0:T(128)S(1)} %copy-done.1, bf16[1024,512]{1,0:T(8,128)(2,1)S(1)} %get-tuple-element.152.refs_2_.refs_6_, bf16[1024,1536]{1,0:T(8,128)(2,1)S(1)} %get-tuple-element.153.refs_3_, ...), custom_call_target="tpu_custom_call" | custom-call | flops 6347999744 | tf_op jit(solution)/shard_map/attention_back/pallas_call | solution.py:80
  84.9 3.2 %attention_back.5 = (bf16[1024,384]{1,0:T(8,128)(2,1)S(1)}, f32[512,384]{1,0:T(8,128)S(1)}) custom-call(s32[1]{0:T(128)} %bitcast.refs_0_, s32[4]{0:T(128)S(1)} %copy-done.1, bf16[1024,512]{1,0:T(8,128)(2,1)S(1)} %get-tuple-element.152.refs_2_.refs_6_, bf16[1024,1536]{1,0:T(8,128)(2,1)S(1)} %get-tuple-element.153.refs_3_, ...), custom_call_target="tpu_custom_call" | custom-call | flops 6347999744 | tf_op jit(solution)/shard_map/attention_back/pallas_call | solution.py:80
  91.1 2.4 %attention_back.7.refs_12_ = bf16[1024,384]{1,0:T(8,128)(2,1)S(1)} custom-call(s32[1]{0:T(128)} %bitcast.refs_0_, s32[4]{0:T(128)S(1)} %copy-done.1, bf16[1024,512]{1,0:T(8,128)(2,1)S(1)} %get-tuple-element.152.refs_2_.refs_6_, bf16[1024,1536]{1,0:T(8,128)(2,1)S(1)} %get-tuple-element.153.refs_3_, f32[4,4,512]{2,1,0:T(4,128)S(1)} %get-tuple-element.146.refs_4_, ...), custom_call_target="tpu_custom_call" | custom-call | flops 6347999744 | tf_op jit(solution)/shard_map/attention_back/pallas_call | solution.py:80
  95.0 4.7 %input_back.1 = (f32[1024,512]{1,0:T(8,128)S(1)}, f32[256,896]{1,0:T(8,128)S(1)}, bf16[256,896]{1,0:T(8,128)(2,1)S(1)}) custom-call(s32[1]{0:T(128)} %bitcast.refs_0_, s32[4]{0:T(128)S(1)} %copy-done.2, s32[4,1,256]{2,1,0:T(1,128)S(1)} %reshape.50.refs_3_.refs_2_, bf16[1024,512]{1,0:T(8,128)(2,1)S(1)} %bitcast.8, ...), custom_call_target="tpu_custom_call" | custom-call | flops 8970000384 | tf_op jit(solution)/shard_map/input_back/pallas_call | solution.py:80
  102.4 2.7 %collective-permute-start.33 = (bf16[16,5376]{1,0:T(8,128)(2,1)S(1)}, bf16[16,5376]{1,0:T(8,128)(2,1)S(1)}, u32[]{:S(2)}, u32[]{:S(2)}) collective-permute-start(bf16[16,5376]{1,0:T(8,128)(2,1)S(1)} %get-tuple-element.249), channel_id=1, source_target_pairs={{0,24},{1,25},{2,26},{3,27},{4,28},{5,29},{6,30},{7,31},{8,16},{9,... | collective-permute-start | bytes 516104 | tf_op jit(solution)/shard_map/ppermute | solution.py:662
  110.2 2.8 %collective-permute-done.34.taken_ref = bf16[128,896]{1,0:T(8,128)(2,1)S(1)} collective-permute-done((bf16[128,896]{1,0:T(8,128)(2,1)S(1)}, bf16[128,896]{1,0:T(8,128)(2,1)S(1)}, u32[]{:S(2)}, u32[]{:S(2)}) %collective-permute-start.34) | collective-permute-done | bytes 229408 | tf_op jit(solution)/shard_map/ppermute | solution.py:662
  114.3 4.7 %collective-permute-done.32.refs_2_ = bf16[16,5376]{1,0:T(8,128)(2,1)S(1)} collective-permute-done((bf16[16,5376]{1,0:T(8,128)(2,1)S(1)}, bf16[16,5376]{1,0:T(8,128)(2,1)S(1)}, u32[]{:S(2)}, u32[]{:S(2)}) %collective-permute-start.32) | collective-permute-done | bytes 172064 | tf_op jit(solution)/shard_map/ppermute | solution.py:662
  119.1 2.9 %collective-permute-start.38 = (bf16[16,896]{1,0:T(8,128)(2,1)S(1)}, bf16[16,896]{1,0:T(8,128)(2,1)S(1)}, u32[]{:S(2)}, u32[]{:S(2)}) collective-permute-start(bf16[16,896]{1,0:T(8,128)(2,1)S(1)} %get-tuple-element.252), channel_id=1, source_target_pairs={{0,24},{1,25},{2,26},{3,27},{4,28},{5,29},{6,30},{7,31},{8,16},{9,... | collective-permute-start | bytes 86024 | tf_op jit(solution)/shard_map/ppermute | solution.py:662
  123.7 2.7 %hidden_update.1 = (f32[16,2048]{1,0:T(8,128)}, f32[16,2048]{1,0:T(8,128)}, f32[16,2048]{1,0:T(8,128)}, f32[64,512]{1,0:T(8,128)}, f32[64,512]{1,0:T(8,128)}, /*...) custom-call(f32[64,5376]{1,0:T(8,128)S(1)} %pad_maximum_fusion.refs_0_, ...), custom_call_target="tpu_custom_call" | custom-call | flops 4140000000 | tf_op jit(solution)/shard_map/hidden_update/pallas_call | solution.py:608
  (151 shorter events, 43.5 us)
Async XLA Ops:
  2.2 7.4 %collective-permute-start.2 = (bf16[16,1664]{1,0:T(8,128)(2,1)S(1)}, bf16[16,1664]{1,0:T(8,128)(2,1)S(1)}, u32[]{:S(2)}, u32[]{:S(2)}) collective-permute-start(bf16[16,1664]{1,0:T(8,128)(2,1)S(1)} %get-tuple-element.133), channel_id=1, source_target_pairs={{0,24},{1,25},{2,26},{3,27},{4,28},{5,29},{6,30},{7,31},{8,16},{9,... | collective-permute-start | bytes 159752 | tf_op jit(solution)/shard_map/ppermute | solution.py:662
  14.0 7.2 %collective-permute-start.14 = (bf16[16,2560]{1,0:T(8,128)(2,1)S(1)}, bf16[16,2560]{1,0:T(8,128)(2,1)S(1)}, u32[]{:S(2)}, u32[]{:S(2)}) collective-permute-start(bf16[16,2560]{1,0:T(8,128)(2,1)S(1)} %slice.31), channel_id=1, source_target_pairs={{0,24},{1,25},{2,26},{3,27},{4,28},{5,29},{6,30},{7,31},{8,16},{9,... | collective-permute-start | bytes 245768 | tf_op jit(solution)/shard_map/ppermute | solution.py:662
  16.5 7.7 %collective-permute-start.13 = (bf16[16,2560]{1,0:T(8,128)(2,1)S(1)}, bf16[16,2560]{1,0:T(8,128)(2,1)S(1)}, u32[]{:S(2)}, u32[]{:S(2)}) collective-permute-start(bf16[16,2560]{1,0:T(8,128)(2,1)S(1)} %slice.31), channel_id=1, source_target_pairs={{0,16},{1,17},{2,18},{3,19},{4,20},{5,21},{6,22},{7,23},{8,24},{9,... | collective-permute-start | bytes 245768 | tf_op jit(solution)/shard_map/ppermute | solution.py:662
  16.5 7.7 %collective-permute-start.12 = (bf16[16,2560]{1,0:T(8,128)(2,1)S(1)}, bf16[16,2560]{1,0:T(8,128)(2,1)S(1)}, u32[]{:S(2)}, u32[]{:S(2)}) collective-permute-start(bf16[16,2560]{1,0:T(8,128)(2,1)S(1)} %slice.31), channel_id=1, source_target_pairs={{0,8},{1,9},{2,10},{3,11},{4,12},{5,13},{6,14},{7,15},{8,0},{9,1},... | collective-permute-start | bytes 245768 | tf_op jit(solution)/shard_map/ppermute | solution.py:662
  18.5 7.3 %collective-permute-start.4 = (bf16[64,1664]{1,0:T(8,128)(2,1)S(1)}, bf16[64,1664]{1,0:T(8,128)(2,1)S(1)}, u32[]{:S(2)}, u32[]{:S(2)}) collective-permute-start(bf16[64,1664]{1,0:T(8,128)(2,1)S(1)} %collective-permute-done.3), channel_id=1, source_target_pairs={{0,1},{1,0},{2,3},{3,2},{4,5},{5,4},{6,7},{7,6},{8,9},{9,8},{10,11... | collective-permute-start | bytes 638984 | tf_op jit(solution)/shard_map/ppermute | solution.py:662
  18.6 11.7 %collective-permute-start.6 = (bf16[128,1664]{1,0:T(8,128)(2,1)S(1)}, bf16[128,1664]{1,0:T(8,128)(2,1)S(1)}, u32[]{:S(2)}, u32[]{:S(2)}) collective-permute-start(bf16[128,1664]{1,0:T(8,128)(2,1)S(1)} %constant_dynamic-update-slice_fusion.refs_5_), channel_id=1, source_target_pairs={{0,2},{1,5},{2,0},{3,7},{4,6},{5,1},{6,4},{7,3},{8,10},{9,13},{10,... | collective-permute-start | bytes 1277960 | tf_op jit(solution)/shard_map/ppermute | solution.py:662
  24.2 7.1 %collective-permute-start.15 = (bf16[64,2560]{1,0:T(8,128)(2,1)S(1)}, bf16[64,2560]{1,0:T(8,128)(2,1)S(1)}, u32[]{:S(2)}, u32[]{:S(2)}) collective-permute-start(bf16[64,2560]{1,0:T(8,128)(2,1)S(1)} %pad_maximum_fusion.3), channel_id=1, source_target_pairs={{0,4},{1,3},{2,6},{3,1},{4,0},{5,7},{6,2},{7,5},{8,12},{9,11},{10,... | collective-permute-start | bytes 983048 | tf_op jit(solution)/shard_map/ppermute | solution.py:662
  25.8 11.8 %collective-permute-start.10 = (bf16[16,2048]{1,0:T(8,128)(2,1)S(1)}, bf16[16,2048]{1,0:T(8,128)(2,1)S(1)}, u32[]{:S(2)}, u32[]{:S(2)}) collective-permute-start(bf16[16,2048]{1,0:T(8,128)(2,1)S(1)} %slice.30), channel_id=1, source_target_pairs={{0,24},{1,25},{2,26},{3,27},{4,28},{5,29},{6,30},{7,31},{8,16},{9,... | collective-permute-start | bytes 196616 | tf_op jit(solution)/shard_map/ppermute | solution.py:662
  28.5 9.1 %collective-permute-start.9 = (bf16[16,2048]{1,0:T(8,128)(2,1)S(1)}, bf16[16,2048]{1,0:T(8,128)(2,1)S(1)}, u32[]{:S(2)}, u32[]{:S(2)}) collective-permute-start(bf16[16,2048]{1,0:T(8,128)(2,1)S(1)} %slice.30), channel_id=1, source_target_pairs={{0,16},{1,17},{2,18},{3,19},{4,20},{5,21},{6,22},{7,23},{8,24},{9,... | collective-permute-start | bytes 196616 | tf_op jit(solution)/shard_map/ppermute | solution.py:662
  28.5 9.1 %collective-permute-start.5 = (bf16[16,2048]{1,0:T(8,128)(2,1)S(1)}, bf16[16,2048]{1,0:T(8,128)(2,1)S(1)}, u32[]{:S(2)}, u32[]{:S(2)}) collective-permute-start(bf16[16,2048]{1,0:T(8,128)(2,1)S(1)} %slice.30), channel_id=1, source_target_pairs={{0,8},{1,9},{2,10},{3,11},{4,12},{5,13},{6,14},{7,15},{8,0},{9,1},... | collective-permute-start | bytes 196616 | tf_op jit(solution)/shard_map/ppermute | solution.py:662
  31.4 14.0 %collective-permute-start.17 = (bf16[128,2560]{1,0:T(8,128)(2,1)S(1)}, bf16[128,2560]{1,0:T(8,128)(2,1)S(1)}, u32[]{:S(2)}, u32[]{:S(2)}) collective-permute-start(bf16[128,2560]{1,0:T(8,128)(2,1)S(1)} %constant_dynamic-update-slice_fusion.5.refs_7_.refs_4_), channel_id=1, source_target_pairs={{0,1},{1,0},{2,3},{3,2},{4,5},{5,4},{6,7},{7,6},{8,9},{9,8},{10,11... | collective-permute-start | bytes 1966088 | tf_op jit(solution)/shard_map/ppermute | solution.py:662
  32.2 13.2 %collective-permute-start.16 = (bf16[128,2560]{1,0:T(8,128)(2,1)S(1)}, bf16[128,2560]{1,0:T(8,128)(2,1)S(1)}, u32[]{:S(2)}, u32[]{:S(2)}) collective-permute-start(bf16[128,2560]{1,0:T(8,128)(2,1)S(1)} %constant_dynamic-update-slice_fusion.5.refs_7_.refs_4_), channel_id=1, source_target_pairs={{0,2},{1,5},{2,0},{3,7},{4,6},{5,1},{6,4},{7,3},{8,10},{9,13},{10,... | collective-permute-start | bytes 1966088 | tf_op jit(solution)/shard_map/ppermute | solution.py:662
  37.7 7.7 %collective-permute-start.11 = (bf16[64,2048]{1,0:T(8,128)(2,1)S(1)}, bf16[64,2048]{1,0:T(8,128)(2,1)S(1)}, u32[]{:S(2)}, u32[]{:S(2)}) collective-permute-start(bf16[64,2048]{1,0:T(8,128)(2,1)S(1)} %pad_maximum_fusion.4), channel_id=1, source_target_pairs={{0,4},{1,3},{2,6},{3,1},{4,0},{5,7},{6,2},{7,5},{8,12},{9,11},{10,... | collective-permute-start | bytes 786440 | tf_op jit(solution)/shard_map/ppermute | solution.py:662
  45.4 7.8 %collective-permute-start.21 = (bf16[128,2048]{1,0:T(8,128)(2,1)S(1)}, bf16[128,2048]{1,0:T(8,128)(2,1)S(1)}, u32[]{:S(2)}, u32[]{:S(2)}) collective-permute-start(bf16[128,2048]{1,0:T(8,128)(2,1)S(1)} %constant_dynamic-update-slice_fusion.10.refs_4_), channel_id=1, source_target_pairs={{0,1},{1,0},{2,3},{3,2},{4,5},{5,4},{6,7},{7,6},{8,9},{9,8},{10,11... | collective-permute-start | bytes 1572872 | tf_op jit(solution)/shard_map/ppermute | solution.py:662
  46.0 9.2 %collective-permute-start.20 = (bf16[128,2048]{1,0:T(8,128)(2,1)S(1)}, bf16[128,2048]{1,0:T(8,128)(2,1)S(1)}, u32[]{:S(2)}, u32[]{:S(2)}) collective-permute-start(bf16[128,2048]{1,0:T(8,128)(2,1)S(1)} %constant_dynamic-update-slice_fusion.10.refs_4_), channel_id=1, source_target_pairs={{0,2},{1,5},{2,0},{3,7},{4,6},{5,1},{6,4},{7,3},{8,10},{9,13},{10,... | collective-permute-start | bytes 1572872 | tf_op jit(solution)/shard_map/ppermute | solution.py:662
  64.1 9.2 %collective-permute-start.24 = (bf16[128,2048]{1,0:T(8,128)(2,1)S(1)}, bf16[128,2048]{1,0:T(8,128)(2,1)S(1)}, u32[]{:S(2)}, u32[]{:S(2)}) collective-permute-start(bf16[128,2048]{1,0:T(8,128)(2,1)S(1)} %get-tuple-element.167), channel_id=1, source_target_pairs={{0,2},{1,5},{2,0},{3,7},{4,6},{5,1},{6,4},{7,3},{8,10},{9,13},{10,... | collective-permute-start | bytes 1572872 | tf_op jit(solution)/shard_map/ppermute | solution.py:662
  72.8 7.2 %collective-permute-start.23 = (bf16[256,2560]{1,0:T(8,128)(2,1)S(1)}, bf16[256,2560]{1,0:T(8,128)(2,1)S(1)}, u32[]{:S(2)}, u32[]{:S(2)}) collective-permute-start(bf16[256,2560]{1,0:T(8,128)(2,1)S(1)} %get-tuple-element.178), channel_id=1, source_target_pairs={{0,1},{1,0},{2,3},{3,2},{4,5},{5,4},{6,7},{7,6},{8,9},{9,8},{10,11... | collective-permute-start | bytes 3932168 | tf_op jit(solution)/shard_map/ppermute | solution.py:662
  80.2 10.7 %collective-permute-start.25 = (bf16[128,2560]{1,0:T(8,128)(2,1)S(1)}, bf16[128,2560]{1,0:T(8,128)(2,1)S(1)}, u32[]{:S(2)}, u32[]{:S(2)}) collective-permute-start(bf16[128,2560]{1,0:T(8,128)(2,1)S(1)} %get-tuple-element.185), channel_id=1, source_target_pairs={{0,2},{1,5},{2,0},{3,7},{4,6},{5,1},{6,4},{7,3},{8,10},{9,13},{10,... | collective-permute-start | bytes 1966088 | tf_op jit(solution)/shard_map/ppermute | solution.py:662
  94.0 8.2 %collective-permute-start.30 = (bf16[64,3328]{1,0:T(8,128)(2,1)S(1)}, bf16[64,3328]{1,0:T(8,128)(2,1)S(1)}, u32[]{:S(2)}, u32[]{:S(2)}) collective-permute-start(bf16[64,3328]{1,0:T(8,128)(2,1)S(1)} %pad_maximum_fusion.2), channel_id=1, source_target_pairs={{0,4},{1,3},{2,6},{3,1},{4,0},{5,7},{6,2},{7,5},{8,12},{9,11},{10,... | collective-permute-start | bytes 1277960 | tf_op jit(solution)/shard_map/ppermute | solution.py:662
  99.7 7.2 %collective-permute-start.29 = (bf16[256,896]{1,0:T(8,128)(2,1)S(1)}, bf16[256,896]{1,0:T(8,128)(2,1)S(1)}, u32[]{:S(2)}, u32[]{:S(2)}) collective-permute-start(bf16[256,896]{1,0:T(8,128)(2,1)S(1)} %get-tuple-element.208), channel_id=1, source_target_pairs={{0,1},{1,0},{2,3},{3,2},{4,5},{5,4},{6,7},{7,6},{8,9},{9,8},{10,11... | collective-permute-start | bytes 1376264 | tf_op jit(solution)/shard_map/ppermute | solution.py:662
  102.4 11.9 %collective-permute-start.33 = (bf16[16,5376]{1,0:T(8,128)(2,1)S(1)}, bf16[16,5376]{1,0:T(8,128)(2,1)S(1)}, u32[]{:S(2)}, u32[]{:S(2)}) collective-permute-start(bf16[16,5376]{1,0:T(8,128)(2,1)S(1)} %get-tuple-element.249), channel_id=1, source_target_pairs={{0,24},{1,25},{2,26},{3,27},{4,28},{5,29},{6,30},{7,31},{8,16},{9,... | collective-permute-start | bytes 516104 | tf_op jit(solution)/shard_map/ppermute | solution.py:662
  105.1 13.9 %collective-permute-start.32 = (bf16[16,5376]{1,0:T(8,128)(2,1)S(1)}, bf16[16,5376]{1,0:T(8,128)(2,1)S(1)}, u32[]{:S(2)}, u32[]{:S(2)}) collective-permute-start(bf16[16,5376]{1,0:T(8,128)(2,1)S(1)} %get-tuple-element.250), channel_id=1, source_target_pairs={{0,16},{1,17},{2,18},{3,19},{4,20},{5,21},{6,22},{7,23},{8,24},{9,... | collective-permute-start | bytes 516104 | tf_op jit(solution)/shard_map/ppermute | solution.py:662
  105.1 13.9 %collective-permute-start.31 = (bf16[16,5376]{1,0:T(8,128)(2,1)S(1)}, bf16[16,5376]{1,0:T(8,128)(2,1)S(1)}, u32[]{:S(2)}, u32[]{:S(2)}) collective-permute-start(bf16[16,5376]{1,0:T(8,128)(2,1)S(1)} %get-tuple-element.251), channel_id=1, source_target_pairs={{0,8},{1,9},{2,10},{3,11},{4,12},{5,13},{6,14},{7,15},{8,0},{9,1},... | collective-permute-start | bytes 516104 | tf_op jit(solution)/shard_map/ppermute | solution.py:662
  119.1 7.3 %collective-permute-start.38 = (bf16[16,896]{1,0:T(8,128)(2,1)S(1)}, bf16[16,896]{1,0:T(8,128)(2,1)S(1)}, u32[]{:S(2)}, u32[]{:S(2)}) collective-permute-start(bf16[16,896]{1,0:T(8,128)(2,1)S(1)} %get-tuple-element.252), channel_id=1, source_target_pairs={{0,24},{1,25},{2,26},{3,27},{4,28},{5,29},{6,30},{7,31},{8,16},{9,... | collective-permute-start | bytes 86024 | tf_op jit(solution)/shard_map/ppermute | solution.py:662
  (35 other events, 251.8 us)
